TPU v7x, 128 devices: a whole 4x4x4 slice. The times are simulated.
128 devices in a mesh: section: 2 (over x_hi), view: 16 (over x_lo, y, core), dp: 4 (over z).
Axes of the slice: x: 4 (x_hi: 2, x_lo: 2; x = x_hi * 2 + x_lo), y: 4, z: 4, core: 2. Of those that a mesh axis runs over, the one named last changes fastest.
Arguments:
- scenes: bfloat16 [8, 16, 128, 1024], P('dp', 'view'), may hold values from -6 to 6
- neighbours: int32 [8, 16, 3], P('dp', 'view'), may hold values from 0 to 15, as said below
- counts: int32 [8, 16], P('dp', 'view'), may hold values from 1 to 3, as said below
- w_in: bfloat16 [2, 1024, 3072], P('section'), may hold values from -8 to 8
- w_out: bfloat16 [2, 1024, 1024], P('section'), may hold values from -1.5 to 1.5
- cotangent: bfloat16 [8, 16, 128, 1024], P('dp', 'view'), may hold values from -3 to 3
Outputs:
- section_outputs: bfloat16 [2, 8, 16, 128, 1024], P('section', 'dp', 'view')
- input_grads: bfloat16 [2, 8, 16, 128, 1024], P('section', 'dp', 'view')
- grad_w_in: float32 [2, 1024, 3072], P('section', ('view', 'dp'))
- grad_w_out: float32 [2, 1024, 1024], P('section', ('view', 'dp'))
Inputs may be any that keep to these rules, and one draw needn't show every extreme that they name: In slots below the view's count, neighbours names distinct views at cycle distance 1 to 2 from the view (index difference modulo 16); the other slots name the view itself. `counts`: in every scene some view has 3 live slots.
All inputs are finite; a program needn't handle non-finite values.
Results may differ from a plain program's by a relative error of at most 0.028.
Values may be sent and summed in bfloat16 or wider, within the bound.
A program may use at most 128 MiB of HBM per device.

v0:
```python
import math

import jax
import jax.numpy as jnp
from jax import lax
from jax.sharding import PartitionSpec as P

HEADS = 8
HEAD_DIM = 128


EPSILON = 1e-06
NEGATIVE = -1e30


def from_behind(value, axis, steps):
    count = lax.axis_size(axis)
    pairs = [(source, (source + steps) % count) for source in range(count)]
    return lax.ppermute(value, axis, pairs)


def from_behind_2(block, axis, distance):
    devices = range(lax.axis_size(axis))
    route = [(i - distance, i) for i in devices if i - distance in devices]
    return lax.ppermute(block, axis, route)


def attend_rows(queries, blocks, block_live, token_rows, model_width):
    block_total = blocks.shape[0]
    key_rows = blocks[..., :model_width].reshape(block_total * token_rows, HEADS, HEAD_DIM)
    value_rows = blocks[..., model_width:].reshape(block_total * token_rows, HEADS, HEAD_DIM)
    query_heads = queries.reshape(token_rows, HEADS, HEAD_DIM)
    key_scale = 1.0 / math.sqrt(HEAD_DIM)
    scores = (
        jnp.einsum("nhe,khe->hnk", query_heads, key_rows, preferred_element_type=jnp.float32)
        * key_scale
    )
    key_live = jnp.repeat(block_live, token_rows)[None, None, :]
    masked = jnp.where(key_live, scores, NEGATIVE)
    row_max = jnp.max(masked, -1, keepdims=True)
    exp_terms = jnp.where(key_live, jnp.exp(masked - row_max), 0.0)
    attn_prob = exp_terms / jnp.sum(exp_terms, -1, keepdims=True)
    prob_low = attn_prob.astype(jnp.bfloat16)
    attended = jnp.einsum("hnk,khe->nhe", prob_low, value_rows, preferred_element_type=jnp.float32)
    return (attn_prob, attended.reshape(token_rows, model_width).astype(jnp.bfloat16))


def take_tick(stacked, position):
    return lax.dynamic_index_in_dim(stacked, position, 0, keepdims=False)


def on_device(scenes, neighbours, counts, w_in, w_out, cotangent):
    view_total = lax.axis_size("view")
    section_total = lax.axis_size("section")
    reach = min(2, (view_total - 1) // 2)
    offsets = list(range(-reach, 0)) + list(range(1, reach + 1))
    micro_total = scenes.shape[0]
    token_rows = scenes.shape[2]
    model_width = scenes.shape[3]
    slot_total = neighbours.shape[2]
    tick_total = micro_total + section_total - 1
    section_no = lax.axis_index("section")
    view_no = lax.axis_index("view")
    weight_in = w_in[0]
    weight_out = w_out[0]
    key_scale = 1.0 / math.sqrt(HEAD_DIM)
    view_rel = (neighbours[:, 0, :] - view_no) % view_total
    signed_rel = jnp.where(view_rel <= reach, view_rel, view_rel - view_total)
    slot_place = jnp.where(signed_rel < 0, signed_rel + reach, signed_rel + reach - 1)
    slot_live = jnp.arange(slot_total, dtype=jnp.int32)[None, :] < counts
    slot_pick = (slot_place[..., None] == jnp.arange(2 * reach, dtype=jnp.int32)) & slot_live[
        ..., None
    ]
    incoming = jnp.zeros((token_rows, model_width), jnp.bfloat16)
    input_list, factor_list, normed_list, query_list = ([], [], [], [])
    block_list, live_list, prob_list, attended_list, output_list = ([], [], [], [], [])
    for tick_no in range(tick_total):
        micro_index = jnp.clip(tick_no - section_no, 0, micro_total - 1)
        first_rows = scenes[min(tick_no, micro_total - 1), 0]
        section_input = jnp.where(section_no == 0, first_rows, incoming)
        upcast = section_input.astype(jnp.float32)
        factor = lax.rsqrt(jnp.mean(upcast * upcast, -1, keepdims=True) + EPSILON)
        normed = (upcast * factor).astype(jnp.bfloat16)
        projected = jnp.dot(normed, weight_in, preferred_element_type=jnp.float32).astype(
            jnp.bfloat16
        )
        queries = projected[:, :model_width]
        keyval = projected[:, model_width:]
        fetched = []
        for offset in offsets:
            fetched.append(from_behind(keyval, "view", -offset))
        candidates = jnp.stack(fetched)
        place_now = take_tick(slot_place, micro_index)
        live_now = take_tick(slot_live, micro_index)
        remote = jnp.take(candidates, place_now, axis=0)
        blocks = jnp.concatenate([keyval[None], remote], 0)
        block_live = jnp.concatenate([jnp.ones((1,), dtype=bool), live_now], 0)
        attn_prob, attended = attend_rows(queries, blocks, block_live, token_rows, model_width)
        branch = jnp.dot(attended, weight_out, preferred_element_type=jnp.float32)
        section_output = (upcast + branch).astype(jnp.bfloat16)
        incoming = from_behind_2(section_output, "section", 1)
        input_list.append(section_input)
        factor_list.append(factor)
        normed_list.append(normed)
        query_list.append(queries)
        block_list.append(blocks)
        live_list.append(block_live)
        prob_list.append(attn_prob)
        attended_list.append(attended)
        output_list.append(section_output)
    input_stack = jnp.stack(input_list)
    factor_stack = jnp.stack(factor_list)
    query_stack = jnp.stack(query_list)
    block_stack = jnp.stack(block_list)
    prob_stack = jnp.stack(prob_list)
    incoming_grad = jnp.zeros((token_rows, model_width), jnp.bfloat16)
    grad_list, proj_list, outgrad_list = ([], [], [])
    for tick_no in range(tick_total):
        micro_index = jnp.clip(tick_no - (section_total - 1 - section_no), 0, micro_total - 1)
        saved_tick = jnp.clip(tick_no - section_total + 1 + 2 * section_no, 0, tick_total - 1)
        section_input = take_tick(input_stack, saved_tick)
        factor = take_tick(factor_stack, saved_tick)
        queries = take_tick(query_stack, saved_tick)
        blocks = take_tick(block_stack, saved_tick)
        attn_prob = take_tick(prob_stack, saved_tick)
        block_total = blocks.shape[0]
        last_rows = take_tick(cotangent[:, 0], micro_index)
        out_grad = jnp.where(section_no == section_total - 1, last_rows, incoming_grad)
        attn_grad = jnp.einsum(
            "nf,df->nd", out_grad, weight_out, preferred_element_type=jnp.float32
        ).astype(jnp.bfloat16)
        grad_heads = attn_grad.reshape(token_rows, HEADS, HEAD_DIM)
        key_rows = blocks[..., :model_width].reshape(block_total * token_rows, HEADS, HEAD_DIM)
        value_rows = blocks[..., model_width:].reshape(block_total * token_rows, HEADS, HEAD_DIM)
        query_heads = queries.reshape(token_rows, HEADS, HEAD_DIM)
        prob_grad = jnp.einsum(
            "nhe,khe->hnk", grad_heads, value_rows, preferred_element_type=jnp.float32
        )
        row_dot = jnp.sum(attn_prob * prob_grad, -1, keepdims=True)
        score_grad = (attn_prob * (prob_grad - row_dot) * key_scale).astype(jnp.bfloat16)
        query_grad = jnp.einsum(
            "hnk,khe->nhe", score_grad, key_rows, preferred_element_type=jnp.float32
        )
        query_grad = query_grad.reshape(token_rows, model_width).astype(jnp.bfloat16)
        key_part = jnp.einsum(
            "hnk,nhe->khe", score_grad, query_heads, preferred_element_type=jnp.float32
        )
        prob_low = attn_prob.astype(jnp.bfloat16)
        value_part = jnp.einsum(
            "hnk,nhe->khe", prob_low, grad_heads, preferred_element_type=jnp.float32
        )
        keyval_part = jnp.concatenate(
            [
                key_part.reshape(block_total, token_rows, model_width),
                value_part.reshape(block_total, token_rows, model_width),
            ],
            -1,
        )
        remote = keyval_part[1:]
        summed = keyval_part[0]
        pick_now = take_tick(slot_pick, micro_index)
        for place_no, offset in enumerate(offsets):
            chosen_part = jnp.sum(jnp.where(pick_now[:, place_no, None, None], remote, 0.0), 0)
            returned = from_behind(chosen_part.astype(jnp.bfloat16), "view", offset)
            summed = summed + returned.astype(jnp.float32)
        proj_grad = jnp.concatenate([query_grad, summed.astype(jnp.bfloat16)], -1)
        normed_grad = jnp.einsum(
            "nf,df->nd", proj_grad, weight_in, preferred_element_type=jnp.float32
        )
        unit_rows = section_input.astype(jnp.float32) * factor
        inner = jnp.mean(normed_grad * unit_rows, -1, keepdims=True)
        input_grad = (
            out_grad.astype(jnp.float32) + factor * (normed_grad - unit_rows * inner)
        ).astype(jnp.bfloat16)
        incoming_grad = from_behind_2(input_grad, "section", -1)
        grad_list.append(input_grad)
        proj_list.append(proj_grad)
        outgrad_list.append(out_grad)
    back_start = section_total - 1 - section_no
    outputs_now = lax.dynamic_slice_in_dim(jnp.stack(output_list), section_no, micro_total, 0)
    grads_now = lax.dynamic_slice_in_dim(jnp.stack(grad_list), back_start, micro_total, 0)
    normed_all = lax.dynamic_slice_in_dim(
        jnp.stack(normed_list), section_no, micro_total, 0
    ).reshape(-1, model_width)
    attended_all = lax.dynamic_slice_in_dim(
        jnp.stack(attended_list), section_no, micro_total, 0
    ).reshape(-1, model_width)
    proj_all = lax.dynamic_slice_in_dim(jnp.stack(proj_list), back_start, micro_total, 0).reshape(
        -1, 3 * model_width
    )
    outgrad_all = lax.dynamic_slice_in_dim(
        jnp.stack(outgrad_list), back_start, micro_total, 0
    ).reshape(-1, model_width)
    share = 1.0 / (micro_total * lax.axis_size("dp"))
    grad_in = (
        jnp.einsum("nd,nf->df", normed_all, proj_all, preferred_element_type=jnp.float32) * share
    )
    grad_out = (
        jnp.einsum("nd,nf->df", attended_all, outgrad_all, preferred_element_type=jnp.float32)
        * share
    )
    grad_in, grad_out = (
        lax.psum_scatter(grad_in, ("view", "dp"), scatter_dimension=0, tiled=True),
        lax.psum_scatter(grad_out, ("view", "dp"), scatter_dimension=0, tiled=True),
    )
    section_outputs = outputs_now.reshape(1, micro_total, 1, token_rows, model_width)
    input_grads = grads_now.reshape(1, micro_total, 1, token_rows, model_width)
    return (section_outputs, input_grads, grad_in[None], grad_out[None])


def solution(mesh):
    in_specs = (
        P("dp", "view", None, None),
        P("dp", "view", None),
        P("dp", "view"),
        P("section", None, None),
        P("section", None, None),
        P("dp", "view", None, None),
    )
    out_specs = (
        P("section", "dp", "view", None, None),
        P("section", "dp", "view", None, None),
        P("section", ("view", "dp"), None),
        P("section", ("view", "dp"), None),
    )
    return jax.shard_map(
        on_device, mesh=mesh, in_specs=in_specs, out_specs=out_specs, check_vma=False
    )
```

profile of v0, /device:TPU:0, one launch (start us, length us, event | category | flops | bytes accessed | tf_op | source)
XLA Modules:
  0.0 921.4 jit_solution(3595080576907049304)
XLA Ops:
  8.5 3.9 fusion.18
  14.3 3.5 collective-permute-start.2
  17.7 4.2 collective-permute-start.3
  27.0 6.8 collective-permute-done.1
  36.0 3.1 pad_maximum_fusion.8
  39.1 3.4 gather_fusion
  47.8 3.5 fusion.296
  55.1 5.4 collective-permute-start.4
  63.8 4.0 fusion.21
  68.7 2.7 collective-permute-start.7
  78.5 8.3 collective-permute-done.6
  88.6 3.1 collective-permute-done.8
  93.3 3.5 gather_fusion.1
  102.2 3.6 fusion.301
  105.8 3.3 fusion.136
  111.0 6.9 collective-permute-start.9
  120.3 2.8 collective-permute-done.9
  128.6 2.9 collective-permute-start.13
  134.8 7.1 collective-permute-done.11
  144.1 3.1 collective-permute-done.13
  147.2 3.1 pad_maximum_fusion.10
  150.4 3.4 gather_fusion.2
  158.9 2.8 dynamic-slice_bitcast_fusion
  161.9 3.3 fusion.306
  173.5 2.9 reshape.420
  176.4 2.9 copy.53
  179.3 2.7 fusion.295
  183.3 3.6 fusion.2
  186.9 3.2 fusion.35
  191.9 2.9 reshape.419
  194.8 2.9 copy.52
  197.7 4.7 select_reduce_fusion.11
  209.6 7.7 collective-permute-done.14
  217.3 4.5 collective-permute-done.15
  224.5 5.3 fusion.179
  232.8 7.5 collective-permute-done.18
  244.4 3.4 convolution_bitcast_fusion.2
  247.8 3.6 fusion.1
  251.4 3.2 fusion.33
  256.4 2.9 reshape.425
  259.3 2.9 copy.60
  262.3 2.9 reshape.426
  265.2 2.9 copy.61
  268.1 4.8 select_reduce_fusion.7
  272.8 3.9 collective-permute-start.20
  285.5 5.5 collective-permute-done.20
  296.4 5.3 fusion.172
  304.1 7.7 collective-permute-done.23
  312.5 3.1 bitcast_multiply_fusion.1
  326.7 3.5 convolution_bitcast_fusion
  330.2 2.9 reshape.432
  333.1 3.0 copy.69
  336.1 3.7 fusion
  339.7 3.2 fusion.31
  344.8 2.9 reshape.431
  347.7 3.0 copy.68
  350.7 4.9 select_reduce_fusion.3
  355.6 4.5 collective-permute-start.25
  364.5 5.1 collective-permute-done.24
  369.6 5.7 collective-permute-done.25
  380.9 6.7 bitcast_multiply_fusion
  390.4 5.1 fusion.165
  396.9 212.2 %reduce-scatter.5.cloned.1.call-done = f32[16,1024]{1,0:T(8,128)} async-done(((f32[1024,1024]{1,0:T(8,128)}), f32[16,1024]{1,0:T(8,128)}) %reduce-scatter.5.cloned.1.call-update) | async-done | bytes 65552 | tf_op jit(solution)/shard_map/reduce_scatter | solution.py:204
  609.1 305.0 %reduce-scatter.3.cloned.1.call-done = f32[16,3072]{1,0:T(8,128)} async-done(((f32[1024,3072]{1,0:T(8,128)}), f32[16,3072]{1,0:T(8,128)}) %reduce-scatter.3.cloned.1.call-update) | async-done | bytes 196624 | tf_op jit(solution)/shard_map/reduce_scatter | solution.py:203
  (305 shorter events, 134.1 us)
Async XLA Ops:
  7.2 17.6 %copy-start = (bf16[1,1024,1024]{2,1,0:T(8,128)(2,1)S(1)}, bf16[1,1024,1024]{2,1,0:T(8,128)(2,1)}, u32[]{:S(2)}) copy-start(bf16[1,1024,1024]{2,1,0:T(8,128)(2,1)} %param.12) | copy-start | bytes 6291460
  7.2 601.9 %reduce-scatter.5.cloned.1.call-start = ((), (), s32[]{:S(2)}) async-start(), calls=%async_computation.3 | async-start | bytes 4259840 | tf_op jit(solution)/shard_map/reduce_scatter | solution.py:204
  8.5 13.4 %copy-start.76 = (s32[2,1]{0,1:T(1,128)S(1)}, s32[2,1]{0,1:T(1,128)}, u32[]{:S(2)}) copy-start(s32[2,1]{0,1:T(1,128)} %param.10) | copy-start | bytes 28
  8.5 13.5 %copy-start.75 = (s32[2,1,3]{2,1,0:T(1,128)S(1)}, s32[2,1,3]{2,1,0:T(1,128)}, u32[]{:S(2)}) copy-start(s32[2,1,3]{2,1,0:T(1,128)} %param.9) | copy-start | bytes 76
  13.3 11.4 %copy-start.31 = (bf16[2,1,128,1024]{3,2,1,0:T(8,128)(2,1)S(1)}, bf16[2,1,128,1024]{3,2,1,0:T(8,128)(2,1)}, u32[]{:S(2)}) copy-start(bf16[2,1,128,1024]{3,2,1,0:T(8,128)(2,1)} %param.13) | copy-start | bytes 1572868
  14.3 12.7 %collective-permute-start.2 = (bf16[128,2048]{1,0:T(8,128)(2,1)}, bf16[128,2048]{1,0:T(8,128)(2,1)}, u32[]{:S(2)}, u32[]{:S(2)}) collective-permute-start(bf16[128,2048]{1,0:T(8,128)(2,1)} %get-tuple-element.70), channel_id=1, source_target_pairs={{0,60},{4,0},{8,4},{12,8},{16,12},{20,16},{24,20},{28,24},{32,28},... | collective-permute-start | bytes 1572872 | tf_op jit(solution)/shard_map/ppermute | solution.py:19
  17.7 16.1 %collective-permute-start.1 = (bf16[128,2048]{1,0:T(8,128)(2,1)}, bf16[128,2048]{1,0:T(8,128)(2,1)}, u32[]{:S(2)}, u32[]{:S(2)}) collective-permute-start(bf16[128,2048]{1,0:T(8,128)(2,1)} %get-tuple-element.70), channel_id=1, source_target_pairs={{0,4},{4,8},{8,12},{12,16},{16,20},{20,24},{24,28},{28,32},{32,36}... | collective-permute-start | bytes 1572872 | tf_op jit(solution)/shard_map/ppermute | solution.py:19
  17.7 17.2 %collective-permute-start = (bf16[128,2048]{1,0:T(8,128)(2,1)}, bf16[128,2048]{1,0:T(8,128)(2,1)}, u32[]{:S(2)}, u32[]{:S(2)}) collective-permute-start(bf16[128,2048]{1,0:T(8,128)(2,1)} %get-tuple-element.70), channel_id=1, source_target_pairs={{0,8},{4,12},{8,16},{12,20},{16,24},{20,28},{24,32},{28,36},{32,40... | collective-permute-start | bytes 1572872 | tf_op jit(solution)/shard_map/ppermute | solution.py:19
  17.7 18.2 %collective-permute-start.3 = (bf16[128,2048]{1,0:T(8,128)(2,1)}, bf16[128,2048]{1,0:T(8,128)(2,1)}, u32[]{:S(2)}, u32[]{:S(2)}) collective-permute-start(bf16[128,2048]{1,0:T(8,128)(2,1)} %get-tuple-element.70), channel_id=1, source_target_pairs={{0,56},{4,60},{8,0},{12,4},{16,8},{20,12},{24,16},{28,20},{32,24},... | collective-permute-start | bytes 1572872 | tf_op jit(solution)/shard_map/ppermute | solution.py:19
  55.1 8.0 copy-start.52
  55.1 8.5 collective-permute-start.4
  63.8 46.0 %copy-start.9 = (bf16[128,1024]{1,0:T(8,128)(2,1)}, bf16[128,1024]{1,0:T(8,128)(2,1)S(1)}, u32[]{:S(2)}) copy-start(bf16[128,1024]{1,0:T(8,128)(2,1)S(1)} %get-tuple-element.38) | copy-start | bytes 786436
  63.8 12.2 %copy-start.47 = (f32[8,128,512]{2,1,0:T(8,128)S(1)}, f32[8,128,512]{2,1,0:T(8,128)}, u32[]{:S(2)}) copy-start(f32[8,128,512]{2,1,0:T(8,128)} %get-tuple-element.91) | copy-start | bytes 6291460
  68.7 9.8 %collective-permute-start.7 = (bf16[128,2048]{1,0:T(8,128)(2,1)S(1)}, bf16[128,2048]{1,0:T(8,128)(2,1)S(1)}, u32[]{:S(2)}, u32[]{:S(2)}) collective-permute-start(bf16[128,2048]{1,0:T(8,128)(2,1)S(1)} %get-tuple-element.68), channel_id=1, source_target_pairs={{0,60},{4,0},{8,4},{12,8},{16,12},{20,16},{24,20},{28,24},{32,28},... | collective-permute-start | bytes 1572872 | tf_op jit(solution)/shard_map/ppermute | solution.py:19
  71.4 15.4 %collective-permute-start.6 = (bf16[128,2048]{1,0:T(8,128)(2,1)S(1)}, bf16[128,2048]{1,0:T(8,128)(2,1)S(1)}, u32[]{:S(2)}, u32[]{:S(2)}) collective-permute-start(bf16[128,2048]{1,0:T(8,128)(2,1)S(1)} %get-tuple-element.68), channel_id=1, source_target_pairs={{0,4},{4,8},{8,12},{12,16},{16,20},{20,24},{24,28},{28,32},{32,36}... | collective-permute-start | bytes 1572872 | tf_op jit(solution)/shard_map/ppermute | solution.py:19
  71.7 16.9 %collective-permute-start.5 = (bf16[128,2048]{1,0:T(8,128)(2,1)S(1)}, bf16[128,2048]{1,0:T(8,128)(2,1)S(1)}, u32[]{:S(2)}, u32[]{:S(2)}) collective-permute-start(bf16[128,2048]{1,0:T(8,128)(2,1)S(1)} %get-tuple-element.68), channel_id=1, source_target_pairs={{0,8},{4,12},{8,16},{12,20},{16,24},{20,28},{24,32},{28,36},{32,40... | collective-permute-start | bytes 1572872 | tf_op jit(solution)/shard_map/ppermute | solution.py:19
  73.4 18.4 %collective-permute-start.8 = (bf16[128,2048]{1,0:T(8,128)(2,1)S(1)}, bf16[128,2048]{1,0:T(8,128)(2,1)S(1)}, u32[]{:S(2)}, u32[]{:S(2)}) collective-permute-start(bf16[128,2048]{1,0:T(8,128)(2,1)S(1)} %get-tuple-element.68), channel_id=1, source_target_pairs={{0,56},{4,60},{8,0},{12,4},{16,8},{20,12},{24,16},{28,20},{32,24},... | collective-permute-start | bytes 1572872 | tf_op jit(solution)/shard_map/ppermute | solution.py:19
  109.1 8.8 copy-start.5
  109.8 8.1 copy-start.3
  109.8 8.1 copy-start.26
  110.5 12.8 %slice-start = ((s8[6291456]{0:T(1024)(128)(4,1)}), s8[4194304]{0:T(1024)(128)(4,1)S(1)}, s32[]{:S(2)}) async-start(s8[6291456]{0:T(1024)(128)(4,1)} %bitcast.444), calls=%async_computation.4 | async-start | bytes 8388608
  111.0 9.3 %copy-start.64 = (bf16[128,1024]{1,0:T(8,128)(2,1)}, bf16[128,1024]{1,0:T(8,128)(2,1)S(1)}, u32[]{:S(2)}) copy-start(bf16[128,1024]{1,0:T(8,128)(2,1)S(1)} %fusion.75) | copy-start | bytes 786436
  111.0 12.3 %slice-start.1 = ((s8[6291456]{0:T(1024)(128)(4,1)}), s8[2097152]{0:T(1024)(128)(4,1)S(1)}, s32[]{:S(2)}) async-start(s8[6291456]{0:T(1024)(128)(4,1)} %bitcast.444), calls=%async_computation.5 | async-start | bytes 4194304
  111.0 12.1 %collective-permute-start.9 = (bf16[128,1024]{1,0:T(8,128)(2,1)S(1)}, bf16[128,1024]{1,0:T(8,128)(2,1)S(1)}, u32[]{:S(2)}, u32[]{:S(2)}) collective-permute-start(bf16[128,1024]{1,0:T(8,128)(2,1)S(1)} %fusion.75), channel_id=1, source_target_pairs={{0,64},{1,65},{2,66},{3,67},{4,68},{5,69},{6,70},{7,71},{8,72},{9,... | collective-permute-start | bytes 786440 | tf_op jit(solution)/shard_map/ppermute | solution.py:25
  124.4 7.8 copy-start.59
  124.4 7.8 copy-start.62
  125.4 9.5 %collective-permute-start.12 = (bf16[128,2048]{1,0:T(8,128)(2,1)}, bf16[128,2048]{1,0:T(8,128)(2,1)}, u32[]{:S(2)}, u32[]{:S(2)}) collective-permute-start(bf16[128,2048]{1,0:T(8,128)(2,1)} %get-tuple-element.66), channel_id=1, source_target_pairs={{0,60},{4,0},{8,4},{12,8},{16,12},{20,16},{24,20},{28,24},{32,28},... | collective-permute-start | bytes 1572872 | tf_op jit(solution)/shard_map/ppermute | solution.py:19
  126.4 15.5 %collective-permute-start.11 = (bf16[128,2048]{1,0:T(8,128)(2,1)}, bf16[128,2048]{1,0:T(8,128)(2,1)}, u32[]{:S(2)}, u32[]{:S(2)}) collective-permute-start(bf16[128,2048]{1,0:T(8,128)(2,1)} %get-tuple-element.66), channel_id=1, source_target_pairs={{0,4},{4,8},{8,12},{12,16},{16,20},{20,24},{24,28},{28,32},{32,36}... | collective-permute-start | bytes 1572872 | tf_op jit(solution)/shard_map/ppermute | solution.py:19
  126.9 17.2 %collective-permute-start.10 = (bf16[128,2048]{1,0:T(8,128)(2,1)}, bf16[128,2048]{1,0:T(8,128)(2,1)}, u32[]{:S(2)}, u32[]{:S(2)}) collective-permute-start(bf16[128,2048]{1,0:T(8,128)(2,1)} %get-tuple-element.66), channel_id=1, source_target_pairs={{0,8},{4,12},{8,16},{12,20},{16,24},{20,28},{24,32},{28,36},{32,40... | collective-permute-start | bytes 1572872 | tf_op jit(solution)/shard_map/ppermute | solution.py:19
  128.6 18.7 %collective-permute-start.13 = (bf16[128,2048]{1,0:T(8,128)(2,1)}, bf16[128,2048]{1,0:T(8,128)(2,1)}, u32[]{:S(2)}, u32[]{:S(2)}) collective-permute-start(bf16[128,2048]{1,0:T(8,128)(2,1)} %get-tuple-element.66), channel_id=1, source_target_pairs={{0,56},{4,60},{8,0},{12,4},{16,8},{20,12},{24,16},{28,20},{32,24},... | collective-permute-start | bytes 1572872 | tf_op jit(solution)/shard_map/ppermute | solution.py:19
  197.7 8.3 copy-start.10
  197.7 8.3 copy-start.63
  202.4 14.9 %collective-permute-start.14 = (bf16[128,2048]{1,0:T(8,128)(2,1)}, bf16[128,2048]{1,0:T(8,128)(2,1)}, u32[]{:S(2)}, u32[]{:S(2)}) collective-permute-start(bf16[128,2048]{1,0:T(8,128)(2,1)} %get-tuple-element.13), channel_id=1, source_target_pairs={{0,56},{4,60},{8,0},{12,4},{16,8},{20,12},{24,16},{28,20},{32,24},... | collective-permute-start | bytes 1572872 | tf_op jit(solution)/shard_map/ppermute | solution.py:19
  204.4 17.4 %collective-permute-start.15 = (bf16[128,2048]{1,0:T(8,128)(2,1)}, bf16[128,2048]{1,0:T(8,128)(2,1)}, u32[]{:S(2)}, u32[]{:S(2)}) collective-permute-start(bf16[128,2048]{1,0:T(8,128)(2,1)} %get-tuple-element.14), channel_id=1, source_target_pairs={{0,60},{4,0},{8,4},{12,8},{16,12},{20,16},{24,20},{28,24},{32,28},... | collective-permute-start | bytes 1572872 | tf_op jit(solution)/shard_map/ppermute | solution.py:19
  204.4 17.4 %collective-permute-start.16 = (bf16[128,2048]{1,0:T(8,128)(2,1)}, bf16[128,2048]{1,0:T(8,128)(2,1)}, u32[]{:S(2)}, u32[]{:S(2)}) collective-permute-start(bf16[128,2048]{1,0:T(8,128)(2,1)} %get-tuple-element.15), channel_id=1, source_target_pairs={{0,4},{4,8},{8,12},{12,16},{16,20},{20,24},{24,28},{28,32},{32,36}... | collective-permute-start | bytes 1572872 | tf_op jit(solution)/shard_map/ppermute | solution.py:19
  204.9 17.4 %collective-permute-start.17 = (bf16[128,2048]{1,0:T(8,128)(2,1)}, bf16[128,2048]{1,0:T(8,128)(2,1)}, u32[]{:S(2)}, u32[]{:S(2)}) collective-permute-start(bf16[128,2048]{1,0:T(8,128)(2,1)} %get-tuple-element.16), channel_id=1, source_target_pairs={{0,8},{4,12},{8,16},{12,20},{16,24},{20,28},{24,32},{28,36},{32,40... | collective-permute-start | bytes 1572872 | tf_op jit(solution)/shard_map/ppermute | solution.py:19
  209.6 14.9 %copy-start.37 = (bf16[128,1024]{1,0:T(8,128)(2,1)}, bf16[128,1024]{1,0:T(8,128)(2,1)S(1)}, u32[]{:S(2)}) copy-start(bf16[128,1024]{1,0:T(8,128)(2,1)S(1)} %copy.54) | copy-start | bytes 786436
  209.6 14.9 %copy-start.17 = (bf16[3,128,1024]{2,1,0:T(8,128)(2,1)S(1)}, bf16[3,128,1024]{2,1,0:T(8,128)(2,1)}, u32[]{:S(2)}) copy-start(bf16[3,128,1024]{2,1,0:T(8,128)(2,1)} %pad_maximum_fusion.13) | copy-start | bytes 2359300
  230.1 10.2 %collective-permute-start.18 = (bf16[128,1024]{1,0:T(8,128)(2,1)S(1)}, bf16[128,1024]{1,0:T(8,128)(2,1)S(1)}, u32[]{:S(2)}, u32[]{:S(2)}) collective-permute-start(bf16[128,1024]{1,0:T(8,128)(2,1)S(1)} %fusion.183), channel_id=1, source_target_pairs={{64,0},{65,1},{66,2},{67,3},{68,4},{69,5},{70,6},{71,7},{72,8},{73... | collective-permute-start | bytes 786440 | tf_op jit(solution)/shard_map/ppermute | solution.py:25
  232.8 14.9 %copy-start.7 = (bf16[64,8,8,128]{3,2,1,0:T(8,128)(2,1)}, bf16[64,8,8,128]{3,2,1,0:T(8,128)(2,1)S(1)}, u32[]{:S(2)}) copy-start(bf16[64,8,8,128]{3,2,1,0:T(8,128)(2,1)S(1)} %copy.91) | copy-start | bytes 3145732
  272.8 12.7 %collective-permute-start.19 = (bf16[128,2048]{1,0:T(8,128)(2,1)}, bf16[128,2048]{1,0:T(8,128)(2,1)}, u32[]{:S(2)}, u32[]{:S(2)}) collective-permute-start(bf16[128,2048]{1,0:T(8,128)(2,1)} %get-tuple-element.9), channel_id=1, source_target_pairs={{0,56},{4,60},{8,0},{12,4},{16,8},{20,12},{24,16},{28,20},{32,24},... | collective-permute-start | bytes 1572872 | tf_op jit(solution)/shard_map/ppermute | solution.py:19
  272.8 18.3 %collective-permute-start.20 = (bf16[128,2048]{1,0:T(8,128)(2,1)}, bf16[128,2048]{1,0:T(8,128)(2,1)}, u32[]{:S(2)}, u32[]{:S(2)}) collective-permute-start(bf16[128,2048]{1,0:T(8,128)(2,1)} %get-tuple-element.10), channel_id=1, source_target_pairs={{0,60},{4,0},{8,4},{12,8},{16,12},{20,16},{24,20},{28,24},{32,28},... | collective-permute-start | bytes 1572872 | tf_op jit(solution)/shard_map/ppermute | solution.py:19
  276.7 15.9 %collective-permute-start.21 = (bf16[128,2048]{1,0:T(8,128)(2,1)}, bf16[128,2048]{1,0:T(8,128)(2,1)}, u32[]{:S(2)}, u32[]{:S(2)}) collective-permute-start(bf16[128,2048]{1,0:T(8,128)(2,1)} %get-tuple-element.11), channel_id=1, source_target_pairs={{0,4},{4,8},{8,12},{12,16},{16,20},{20,24},{24,28},{28,32},{32,36}... | collective-permute-start | bytes 1572872 | tf_op jit(solution)/shard_map/ppermute | solution.py:19
  276.7 17.4 %collective-permute-start.22 = (bf16[128,2048]{1,0:T(8,128)(2,1)}, bf16[128,2048]{1,0:T(8,128)(2,1)}, u32[]{:S(2)}, u32[]{:S(2)}) collective-permute-start(bf16[128,2048]{1,0:T(8,128)(2,1)} %get-tuple-element.12), channel_id=1, source_target_pairs={{0,8},{4,12},{8,16},{12,20},{16,24},{20,28},{24,32},{28,36},{32,40... | collective-permute-start | bytes 1572872 | tf_op jit(solution)/shard_map/ppermute | solution.py:19
  284.9 11.4 %copy-start.42 = (bf16[128,1024]{1,0:T(8,128)(2,1)}, bf16[128,1024]{1,0:T(8,128)(2,1)S(1)}, u32[]{:S(2)}) copy-start(bf16[128,1024]{1,0:T(8,128)(2,1)S(1)} %copy.62) | copy-start | bytes 786436
  284.9 11.4 %copy-start.18 = (bf16[3,128,1024]{2,1,0:T(8,128)(2,1)S(1)}, bf16[3,128,1024]{2,1,0:T(8,128)(2,1)}, u32[]{:S(2)}) copy-start(bf16[3,128,1024]{2,1,0:T(8,128)(2,1)} %pad_maximum_fusion.13) | copy-start | bytes 2359300
  301.9 9.8 %collective-permute-start.23 = (bf16[128,1024]{1,0:T(8,128)(2,1)S(1)}, bf16[128,1024]{1,0:T(8,128)(2,1)S(1)}, u32[]{:S(2)}, u32[]{:S(2)}) collective-permute-start(bf16[128,1024]{1,0:T(8,128)(2,1)S(1)} %fusion.176), channel_id=1, source_target_pairs={{64,0},{65,1},{66,2},{67,3},{68,4},{69,5},{70,6},{71,7},{72,8},{73... | collective-permute-start | bytes 786440 | tf_op jit(solution)/shard_map/ppermute | solution.py:25
  303.3 8.5 copy-start.33
  303.3 9.2 copy-start.70
  303.3 9.2 copy-start.71
  303.3 9.2 copy-start.73
  304.0 7.7 copy-start.74
  315.6 598.6 %reduce-scatter.3.cloned.1.call-start = ((), (), s32[]{:S(2)}) async-start(), calls=%async_computation.2 | async-start | bytes 12779520 | tf_op jit(solution)/shard_map/reduce_scatter | solution.py:203
  322.3 13.8 %copy-start.6 = (bf16[64,8,8,128]{3,2,1,0:T(8,128)(2,1)}, bf16[64,8,8,128]{3,2,1,0:T(8,128)(2,1)S(1)}, u32[]{:S(2)}) copy-start(bf16[64,8,8,128]{3,2,1,0:T(8,128)(2,1)S(1)} %copy.93) | copy-start | bytes 3145732
  350.7 10.5 %copy-start.24 = (bf16[128,2048]{1,0:T(8,128)(2,1)S(1)}, bf16[128,2048]{1,0:T(8,128)(2,1)}, u32[]{:S(2)}) copy-start(bf16[128,2048]{1,0:T(8,128)(2,1)} %copy-done.23) | copy-start | bytes 1572868
  350.7 10.5 %copy-start.43 = (bf16[128,1024]{1,0:T(8,128)(2,1)S(1)}, bf16[128,1024]{1,0:T(8,128)(2,1)}, u32[]{:S(2)}) copy-start(bf16[128,1024]{1,0:T(8,128)(2,1)} %copy-done.42) | copy-start | bytes 786436
  350.7 11.5 %copy-start.27 = (bf16[64,8,8,128]{3,2,1,0:T(8,128)(2,1)S(1)}, bf16[64,8,8,128]{3,2,1,0:T(8,128)(2,1)}, u32[]{:S(2)}) copy-start(bf16[64,8,8,128]{3,2,1,0:T(8,128)(2,1)} %copy.92) | copy-start | bytes 3145732
  355.6 14.0 %collective-permute-start.24 = (bf16[128,2048]{1,0:T(8,128)(2,1)}, bf16[128,2048]{1,0:T(8,128)(2,1)}, u32[]{:S(2)}, u32[]{:S(2)}) collective-permute-start(bf16[128,2048]{1,0:T(8,128)(2,1)} %get-tuple-element.5), channel_id=1, source_target_pairs={{0,56},{4,60},{8,0},{12,4},{16,8},{20,12},{24,16},{28,20},{32,24},... | collective-permute-start | bytes 1572872 | tf_op jit(solution)/shard_map/ppermute | solution.py:19
  355.6 19.7 %collective-permute-start.25 = (bf16[128,2048]{1,0:T(8,128)(2,1)}, bf16[128,2048]{1,0:T(8,128)(2,1)}, u32[]{:S(2)}, u32[]{:S(2)}) collective-permute-start(bf16[128,2048]{1,0:T(8,128)(2,1)} %get-tuple-element.6), channel_id=1, source_target_pairs={{0,60},{4,0},{8,4},{12,8},{16,12},{20,16},{24,20},{28,24},{32,28},... | collective-permute-start | bytes 1572872 | tf_op jit(solution)/shard_map/ppermute | solution.py:19
  360.1 16.1 %collective-permute-start.26 = (bf16[128,2048]{1,0:T(8,128)(2,1)}, bf16[128,2048]{1,0:T(8,128)(2,1)}, u32[]{:S(2)}, u32[]{:S(2)}) collective-permute-start(bf16[128,2048]{1,0:T(8,128)(2,1)} %get-tuple-element.7), channel_id=1, source_target_pairs={{0,4},{4,8},{8,12},{12,16},{16,20},{20,24},{24,28},{28,32},{32,36}... | collective-permute-start | bytes 1572872 | tf_op jit(solution)/shard_map/ppermute | solution.py:19
  360.1 17.2 %collective-permute-start.27 = (bf16[128,2048]{1,0:T(8,128)(2,1)}, bf16[128,2048]{1,0:T(8,128)(2,1)}, u32[]{:S(2)}, u32[]{:S(2)}) collective-permute-start(bf16[128,2048]{1,0:T(8,128)(2,1)} %get-tuple-element.8), channel_id=1, source_target_pairs={{0,8},{4,12},{8,16},{12,20},{16,24},{20,28},{24,32},{28,36},{32,40... | collective-permute-start | bytes 1572872 | tf_op jit(solution)/shard_map/ppermute | solution.py:19
  364.5 15.2 %copy-start.49 = (bf16[1,128,1024]{2,1,0:T(8,128)(2,1)S(1)}, bf16[1,128,1024]{2,1,0:T(8,128)(2,1)}, u32[]{:S(2)}) copy-start(bf16[1,128,1024]{2,1,0:T(8,128)(2,1)} %fusion.202) | copy-start | bytes 786436
  364.5 15.2 %copy-start.50 = (bf16[1,128,1024]{2,1,0:T(8,128)(2,1)S(1)}, bf16[1,128,1024]{2,1,0:T(8,128)(2,1)}, u32[]{:S(2)}) copy-start(bf16[1,128,1024]{2,1,0:T(8,128)(2,1)} %fusion.200) | copy-start | bytes 786436
  364.5 15.2 %copy-start.51 = (bf16[1,128,1024]{2,1,0:T(8,128)(2,1)S(1)}, bf16[1,128,1024]{2,1,0:T(8,128)(2,1)}, u32[]{:S(2)}) copy-start(bf16[1,128,1024]{2,1,0:T(8,128)(2,1)} %get-tuple-element.29) | copy-start | bytes 786436
  (45 other events, 131.3 us)
Sparse Core Ops, SparseCore 0:
  315.7 293.3 reduce-scatter.4
  612.2 301.8 reduce-scatter.2
where the time goes:
time: 930 us; the launch traced here: 921 us
  waiting for transfers between devices  606 us (65%)
  local copies, waits for them, and re-layouts  96.8 us (10%)
  matrix products  94.1 us (10%)
  other arithmetic  58.7 us (6%)
  starting transfers between devices  50.4 us (5%)
  between operations  15.6 us (2%)
    reduce_scatter x1, waiting for transfers between devices, on_device(): lax.psum_scatter(grad_in, ('view', 'dp'), scatter_dimension=0, tiled=True)  305 us
    reduce_scatter x1, waiting for transfers between devices, on_device(): lax.psum_scatter(grad_out, ('view', 'dp'), scatter_dimension=0, tiled=True)  212 us
    ppermute x24, waiting for transfers between devices, from_behind(): return lax.ppermute(value, axis, pairs)  70 us
    ppermute x24, starting transfers between devices, from_behind(): return lax.ppermute(value, axis, pairs)  35.5 us
    unnamed x170, local copies, waits for them, and re-layouts  24.3 us
  transfers between devices with their start and end apart: 30, of which 27 were waited for; matrix products, arithmetic and copies ran while one was open for 10% of the time, Pallas kernels for 0%

commit v1 on v0

--- a/solution.py
+++ b/solution.py
@@ -1,9 +1,14 @@
+import functools
 import math
 
 import jax
 import jax.numpy as jnp
 from jax import lax
+from jax.experimental import pallas as pl
+from jax.experimental.pallas import tpu as pltpu
 from jax.sharding import PartitionSpec as P
+
+MESH = pl.DeviceIdType.MESH
 
 HEADS = 8
 HEAD_DIM = 128
@@ -11,6 +16,199 @@
 
 EPSILON = 1e-06
 NEGATIVE = -1e30
+
+
+CHUNK = 512
+PAIRS = ((6, 7), (0, 1), (2, 3), (4, 5))
+
+
+def wgrad_kernel(
+    share, nT, aT, proj, og, gin, gout,
+    nT_r, aT_r, proj_r, og_r, G, r1, r2, r3, r4, r5,
+    xs, xr, ss, rs,
+):
+    view = lax.axis_index("view")
+    zi = lax.axis_index("dp")
+    core = lax.rem(view, 2)
+    yi = lax.rem(view // 2, 4)
+    xi = view // 8
+    peer = xi * 8 + yi * 2 + (1 - core)
+    across = (1 - xi) * 8 + yi * 2 + core
+
+    def y_dev(step):
+        return {"view": xi * 8 + lax.rem(yi + step + 4, 4) * 2 + core}
+
+    def z_dev(step):
+        return {"dp": lax.rem(zi + step + 4, 4)}
+
+    barrier = pltpu.get_barrier_semaphore()
+    partners = ({"view": peer}, {"view": across}, y_dev(1), y_dev(-1), z_dev(1), z_dev(-1))
+    for dev in partners:
+        pl.semaphore_signal(barrier, inc=1, device_id=dev, device_id_type=MESH)
+    pl.semaphore_wait(barrier, len(partners))
+
+    def remote(src, dst, s, r, dev):
+        return pltpu.make_async_remote_copy(
+            src_ref=src, dst_ref=dst, send_sem=s, recv_sem=r, device_id=dev, device_id_type=MESH
+        )
+
+    def cols(ref, k):
+        return ref.at[:, pl.ds(k * CHUNK, CHUNK)]
+
+    pieces = {}
+    pieces["a"] = remote(aT.at[:, 1 - core], aT_r, xs.at[8], xr.at[8], {"view": peer})
+    pieces["n"] = remote(nT.at[:, 1 - core], nT_r, xs.at[9], xr.at[9], {"view": peer})
+    for n in range(6):
+        pieces[n] = remote(cols(proj, n), cols(proj_r, n), xs.at[n], xr.at[n], {"view": peer})
+    for n in range(6, 8):
+        pieces[n] = remote(
+            cols(og, n - 6), cols(og_r, n - 6), xs.at[n], xr.at[n], {"view": peer}
+        )
+    for key in ("a", 6, 7, "n", 0, 1, 2, 3, 4, 5):
+        pieces[key].start()
+
+    def first(n, x_at, a):
+        return G.at[n, x_at, a] if n % 2 == 0 else G.at[n, x_at, :, a]
+
+    def second(n, x_at, a, b):
+        return G.at[n, x_at, a, b] if n % 2 == 0 else G.at[n, x_at, b, a]
+
+    whole = slice(None)
+    sent = []
+
+    def send(n, k, src, dst, dev):
+        copy = remote(src, dst, ss.at[n, k], rs.at[n, k], dev)
+        copy.start()
+        sent.append(copy)
+        return copy
+
+    arrived = {}
+
+    def add_into(ref, *others):
+        total = ref[...].astype(jnp.float32)
+        for other in others:
+            total = total + other[...].astype(jnp.float32)
+        ref[...] = total.astype(jnp.bfloat16)
+
+    seen = set()
+
+    def need(key):
+        if key not in seen:
+            seen.add(key)
+            pieces[key].wait_recv()
+
+    def stage(n, s):
+        a, b = (yi, zi) if n % 2 == 0 else (zi, yi)
+        dev1, dev2 = (y_dev, z_dev) if n % 2 == 0 else (z_dev, y_dev)
+        if s == 0:
+            if n >= 6:
+                need("a")
+                left, left_r, right, right_r, k = aT, aT_r, og, og_r, n - 6
+            else:
+                need("n")
+                left, left_r, right, right_r, k = nT, nT_r, proj, proj_r, n
+            need(n)
+            rows = left.shape[0] * left.shape[2]
+            toks = left.shape[3]
+            mine = left[:, core].reshape(rows, toks)
+            theirs = left_r[...].reshape(rows, toks)
+            part = jnp.dot(
+                mine, right[:, k * CHUNK : (k + 1) * CHUNK], preferred_element_type=jnp.float32
+            ) + jnp.dot(
+                theirs, right_r[:, k * CHUNK : (k + 1) * CHUNK], preferred_element_type=jnp.float32
+            )
+            G[n] = part.astype(jnp.bfloat16).reshape(G.shape[1:])
+            opp = lax.rem(a + 2, 4)
+            arrived[n, 0] = (
+                send(n, 0, first(n, 0, opp), r1.at[n, 0], dev1(1)),
+                send(n, 1, first(n, 1, opp), r1.at[n, 1], dev1(-1)),
+            )
+            return
+        for copy in arrived[n, s - 1]:
+            copy.wait_recv()
+        if s == 1:
+            up, down = lax.rem(a + 1, 4), lax.rem(a + 3, 4)
+            add_into(first(n, 0, up), r1.at[n, 0])
+            add_into(first(n, 1, down), r1.at[n, 1])
+            arrived[n, 1] = (
+                send(n, 2, first(n, whole, up), r2.at[n, 0], dev1(1)),
+                send(n, 3, first(n, whole, down), r2.at[n, 1], dev1(-1)),
+            )
+        elif s == 2:
+            add_into(first(n, whole, a), r2.at[n, 0], r2.at[n, 1])
+            opp = lax.rem(b + 2, 4)
+            arrived[n, 2] = (
+                send(n, 4, second(n, 0, a, opp), r3.at[n, 0], dev2(1)),
+                send(n, 5, second(n, 1, a, opp), r3.at[n, 1], dev2(-1)),
+            )
+        elif s == 3:
+            up, down = lax.rem(b + 1, 4), lax.rem(b + 3, 4)
+            add_into(second(n, 0, a, up), r3.at[n, 0])
+            add_into(second(n, 1, a, down), r3.at[n, 1])
+            arrived[n, 3] = (
+                send(n, 6, second(n, whole, a, up), r4.at[n, 0], dev2(1)),
+                send(n, 7, second(n, whole, a, down), r4.at[n, 1], dev2(-1)),
+            )
+        elif s == 4:
+            add_into(second(n, whole, a, b), r4.at[n, 0], r4.at[n, 1])
+            arrived[n, 4] = (
+                send(n, 8, second(n, 1 - xi, a, b), r5.at[n], {"view": across}),
+            )
+        else:
+            total = second(n, xi, a, b)[...].astype(jnp.float32) + r5[n].astype(jnp.float32)
+            out, k = (gin, n) if n < 6 else (gout, n - 6)
+            out[:, k * CHUNK : (k + 1) * CHUNK] = total * share
+
+    stages = 6
+    for turn in range(len(PAIRS) + stages - 1):
+        for p in range(len(PAIRS)):
+            s = turn - p
+            if 0 <= s < stages:
+                for n in PAIRS[p]:
+                    stage(n, s)
+    for copy in list(pieces.values()) + sent:
+        copy.wait_send()
+
+
+def weight_grads(normed, attended, proj, outgrad, share):
+    toks, width = normed.shape
+    chunks = 4 * width // CHUNK
+    nT = normed.T.reshape(8, 2, width // 16, toks)
+    aT = attended.T.reshape(8, 2, width // 16, toks)
+    rows = width // 64
+    vm = pl.BlockSpec(memory_space=pltpu.VMEM)
+    bf = jnp.bfloat16
+    return pl.pallas_call(
+        functools.partial(wgrad_kernel, share),
+        out_shape=(
+            jax.ShapeDtypeStruct((rows, 3 * width), jnp.float32),
+            jax.ShapeDtypeStruct((rows, width), jnp.float32),
+        ),
+        in_specs=[vm] * 4,
+        out_specs=(vm, vm),
+        scratch_shapes=[
+            pltpu.VMEM((8, width // 16, toks), bf),
+            pltpu.VMEM((8, width // 16, toks), bf),
+            pltpu.VMEM((toks, 3 * width), bf),
+            pltpu.VMEM((toks, width), bf),
+            pltpu.VMEM((chunks, 2, 4, 4, rows, CHUNK), bf),
+            pltpu.VMEM((chunks, 2, 4, rows, CHUNK), bf),
+            pltpu.VMEM((chunks, 2, 2, 4, rows, CHUNK), bf),
+            pltpu.VMEM((chunks, 2, rows, CHUNK), bf),
+            pltpu.VMEM((chunks, 2, 2, rows, CHUNK), bf),
+            pltpu.VMEM((chunks, rows, CHUNK), bf),
+            pltpu.SemaphoreType.DMA((10,)),
+            pltpu.SemaphoreType.DMA((10,)),
+            pltpu.SemaphoreType.DMA((chunks, 9)),
+            pltpu.SemaphoreType.DMA((chunks, 9)),
+        ],
+        compiler_params=pltpu.CompilerParams(
+            collective_id=1, has_side_effects=True, vmem_limit_bytes=40 * 1024 * 1024
+        ),
+        cost_estimate=pl.CostEstimate(
+            flops=2 * 512 * 512 * 4096, bytes_accessed=4 << 20, transcendentals=0
+        ),
+    )(nT, aT, proj, outgrad)
 
 
 def from_behind(value, axis, steps):
@@ -192,17 +390,7 @@
         jnp.stack(outgrad_list), back_start, micro_total, 0
     ).reshape(-1, model_width)
     share = 1.0 / (micro_total * lax.axis_size("dp"))
-    grad_in = (
-        jnp.einsum("nd,nf->df", normed_all, proj_all, preferred_element_type=jnp.float32) * share
-    )
-    grad_out = (
-        jnp.einsum("nd,nf->df", attended_all, outgrad_all, preferred_element_type=jnp.float32)
-        * share
-    )
-    grad_in, grad_out = (
-        lax.psum_scatter(grad_in, ("view", "dp"), scatter_dimension=0, tiled=True),
-        lax.psum_scatter(grad_out, ("view", "dp"), scatter_dimension=0, tiled=True),
-    )
+    grad_in, grad_out = weight_grads(normed_all, attended_all, proj_all, outgrad_all, share)
     section_outputs = outputs_now.reshape(1, micro_total, 1, token_rows, model_width)
     input_grads = grads_now.reshape(1, micro_total, 1, token_rows, model_width)
     return (section_outputs, input_grads, grad_in[None], grad_out[None])

time: 930 us -> 435 us (0.47)
  waiting for transfers between devices: 606 us -> 72.2 us
  Pallas kernels: 0 us -> 51.5 us
  between operations: 15.6 us -> 2.23 us
  matrix products: 94.1 us -> 84.5 us
    reduce_scatter x2 -> x0, waiting for transfers between devices: 517 us -> none  [the longest x1 305 us: on_device(): lax.psum_scatter(grad_in, ('view', 'dp'), scatter_dimension=0, tiled=True)]
    pallas_call x0 -> x1, Pallas kernels: none -> 51.5 us  [weight_grads(): pl.pallas_call(functools.partial(wgrad_kernel, share), out_shape=(jax.Sha...]
    ppermute x24, waiting for transfers between devices: 70 us -> 58.1 us  [from_behind(): return lax.ppermute(value, axis, pairs)]
    dot_general x2 -> x0, matrix products: 9.81 us -> none  [the longest x1 6.73 us: on_device(): jnp.einsum('nd,nf->df', normed_all, proj_all, preferred_element_type=jnp....]
    unnamed x170 -> x176, local copies, waits for them, and re-layouts: 24.3 us -> 29.7 us
  transfers between devices with their start and end apart: 30 -> 28, of which waited for: 27 -> 22; matrix products, arithmetic and copies ran while one was open for 10% -> 11% of each run, Pallas kernels for 0% -> 0%
where the time goes in v1:
time: 435 us; the launch traced here: 427 us
  local copies, waits for them, and re-layouts  103 us (24%)
  matrix products  84.5 us (19%)
  waiting for transfers between devices  72.2 us (17%)
  other arithmetic  62.5 us (14%)
  Pallas kernels  51.5 us (12%)
  starting transfers between devices  51.1 us (12%)
    ppermute x24, waiting for transfers between devices, from_behind(): return lax.ppermute(value, axis, pairs)  58.1 us
    pallas_call x1, Pallas kernels, weight_grads(): pl.pallas_call(functools.partial(wgrad_kernel, share), out_shape=(jax.Sha...  51.5 us
    ppermute x24, starting transfers between devices, from_behind(): return lax.ppermute(value, axis, pairs)  36.2 us
    unnamed x176, local copies, waits for them, and re-layouts  29.7 us
    reshape x6, local copies, waits for them, and re-layouts, on_device(): key_part.reshape(block_total, token_rows, model_width)  17.6 us
    reshape x6, local copies, waits for them, and re-layouts, on_device(): value_part.reshape(block_total, token_rows, model_width)  17.5 us
    ppermute x4, starting transfers between devices, from_behind_2(): return lax.ppermute(block, axis, route)  14.8 us
    reduce_sum x3, other arithmetic, on_device(): jnp.sum(jnp.where(pick_now[:, place_no, None, None], remote, 0.0), 0)  14.7 us
  transfers between devices with their start and end apart: 28, of which 22 were waited for; matrix products, arithmetic and copies ran while one was open for 11% of the time, Pallas kernels for 0%

profile of v1, /device:TPU:0, one launch (start us, length us, event | category | flops | bytes accessed | tf_op | source)
XLA Modules:
  0.0 426.7 jit_solution(5088861537831459659)
XLA Ops:
  1.9 4.0 fusion.18
  7.7 3.5 collective-permute-start.2
  11.2 4.2 collective-permute-start.3
  20.5 6.8 %collective-permute-done.1 = bf16[128,2048]{1,0:T(8,128)(2,1)} collective-permute-done((bf16[128,2048]{1,0:T(8,128)(2,1)}, bf16[128,2048]{1,0:T(8,128)(2,1)}, u32[]{:S(2)}, u32[]{:S(2)}) %collective-permute-start.1) | collective-permute-done | bytes 524320 | tf_op jit(solution)/shard_map/ppermute | solution.py:217
  29.5 3.1 pad_maximum_fusion.8
  32.6 3.5 gather_fusion
  41.5 3.5 fusion.289
  44.9 2.6 convolution_convert_fusion.5
  48.8 5.3 %collective-permute-start.4 = (bf16[128,1024]{1,0:T(8,128)(2,1)S(1)}, bf16[128,1024]{1,0:T(8,128)(2,1)}, u32[]{:S(2)}, u32[]{:S(2)}) collective-permute-start(bf16[128,1024]{1,0:T(8,128)(2,1)S(1)} %fusion.77), channel_id=1, source_target_pairs={{0,64},{1,65},{2,66},{3,67},{4,68},{5,69},{6,70},{7,71},{8,72},{9,... | collective-permute-start | bytes 786440 | tf_op jit(solution)/shard_map/ppermute | solution.py:223
  57.5 4.0 fusion.21
  62.3 2.7 collective-permute-start.7
  67.0 2.7 collective-permute-start.8
  72.8 7.7 %collective-permute-done.6 = bf16[128,2048]{1,0:T(8,128)(2,1)S(1)} collective-permute-done((bf16[128,2048]{1,0:T(8,128)(2,1)S(1)}, bf16[128,2048]{1,0:T(8,128)(2,1)S(1)}, u32[]{:S(2)}, u32[]{:S(2)}) %collective-permute-start.6) | collective-permute-done | bytes 524320 | tf_op jit(solution)/shard_map/ppermute | solution.py:217
  82.2 3.1 collective-permute-done.8
  86.9 3.5 gather_fusion.1
  95.8 3.6 fusion.294
  99.4 3.3 fusion.135
  104.6 6.9 %collective-permute-start.9 = (bf16[128,1024]{1,0:T(8,128)(2,1)S(1)}, bf16[128,1024]{1,0:T(8,128)(2,1)S(1)}, u32[]{:S(2)}, u32[]{:S(2)}) collective-permute-start(bf16[128,1024]{1,0:T(8,128)(2,1)S(1)} %fusion.74), channel_id=1, source_target_pairs={{0,64},{1,65},{2,66},{3,67},{4,68},{5,69},{6,70},{7,71},{8,72},{9,... | collective-permute-start | bytes 786440 | tf_op jit(solution)/shard_map/ppermute | solution.py:223
  111.6 2.4 fusion.28
  113.9 2.8 collective-permute-done.9
  123.3 2.9 collective-permute-start.13
  138.9 3.1 collective-permute-done.13
  142.0 3.1 pad_maximum_fusion.10
  145.1 3.4 gather_fusion.2
  153.7 2.5 dynamic-slice_bitcast_fusion
  159.1 3.4 fusion.299
  166.4 2.7 copy-done.1
  170.9 2.9 reshape.434
  173.8 2.9 copy.53
  181.0 3.8 fusion.2
  184.8 3.2 fusion.35
  190.7 2.9 reshape.433
  193.6 2.9 copy.52
  196.6 4.9 %select_reduce_fusion.11 = (bf16[128,2048]{1,0:T(8,128)(2,1)}, bf16[128,2048]{1,0:T(8,128)(2,1)}, bf16[128,2048]{1,0:T(8,128)(2,1)}, bf16[128,2048]{1,0:T(8,128)(2,1)}) fusion(pred[3]{0:T(512)(128)(4,1)S(1)} %get-tuple-element.29, f32[4,128,1024]{2,1,0:T(8,128)} %copy.53, f32[4,128,1024]{2,1,0:T(8,128)} %copy.52, pred[3]{0:T(512)(128)(4,1)S(1)} %get-tuple-element.32, ...), kind=kLoop, calls=%fused_computation.49 | loop fusion | flops 6029312 | bytes 6291468 | tf_op jit(solution)/shard_map/reduce_sum | solution.py:361
  207.1 2.7 convolution_convert_fusion.3
  209.8 6.5 %collective-permute-done.14 = bf16[128,2048]{1,0:T(8,128)(2,1)} collective-permute-done((bf16[128,2048]{1,0:T(8,128)(2,1)}, bf16[128,2048]{1,0:T(8,128)(2,1)}, u32[]{:S(2)}, u32[]{:S(2)}) %collective-permute-start.14) | collective-permute-done | bytes 524320 | tf_op jit(solution)/shard_map/ppermute | solution.py:217
  216.3 4.5 %collective-permute-done.15 = bf16[128,2048]{1,0:T(8,128)(2,1)} collective-permute-done((bf16[128,2048]{1,0:T(8,128)(2,1)}, bf16[128,2048]{1,0:T(8,128)(2,1)}, u32[]{:S(2)}, u32[]{:S(2)}) %collective-permute-start.15) | collective-permute-done | bytes 524320 | tf_op jit(solution)/shard_map/ppermute | solution.py:217
  223.5 2.3 fusion.176
  237.3 3.4 convolution_bitcast_fusion.2
  240.7 3.8 fusion.1
  244.5 3.2 fusion.33
  250.4 2.9 reshape.439
  253.3 2.9 copy.60
  256.2 2.9 reshape.440
  259.2 2.9 copy.61
  262.1 4.9 %select_reduce_fusion.7 = (bf16[128,2048]{1,0:T(8,128)(2,1)}, bf16[128,2048]{1,0:T(8,128)(2,1)}, bf16[128,2048]{1,0:T(8,128)(2,1)}, bf16[128,2048]{1,0:T(8,128)(2,1)}) fusion(pred[3]{0:T(512)(128)(4,1)S(1)} %get-tuple-element.113, f32[4,128,1024]{2,1,0:T(8,128)} %copy.61, f32[4,128,1024]{2,1,0:T(8,128)} %copy.60, pred[3]{0:T(512)(128)(4,1)S(1)} %get-tuple-element.110, ...), kind=kLoop, calls=%fused_computation.45 | loop fusion | flops 6029312 | bytes 6291468 | tf_op jit(solution)/shard_map/reduce_sum | solution.py:361
  267.0 4.4 %collective-permute-start.20 = (bf16[128,2048]{1,0:T(8,128)(2,1)}, bf16[128,2048]{1,0:T(8,128)(2,1)}, u32[]{:S(2)}, u32[]{:S(2)}) collective-permute-start(bf16[128,2048]{1,0:T(8,128)(2,1)} %get-tuple-element.14), channel_id=1, source_target_pairs={{0,60},{4,0},{8,4},{12,8},{16,12},{20,16},{24,20},{28,24},{32,28},... | collective-permute-start | bytes 1572872 | tf_op jit(solution)/shard_map/ppermute | solution.py:217
  277.0 2.4 collective-permute-done.19
  279.4 5.8 %collective-permute-done.20 = bf16[128,2048]{1,0:T(8,128)(2,1)} collective-permute-done((bf16[128,2048]{1,0:T(8,128)(2,1)}, bf16[128,2048]{1,0:T(8,128)(2,1)}, u32[]{:S(2)}, u32[]{:S(2)}) %collective-permute-start.20) | collective-permute-done | bytes 524320 | tf_op jit(solution)/shard_map/ppermute | solution.py:217
  290.9 5.3 %fusion.169 = (f32[128]{0:T(128)S(1)}, f32[128,1024]{1,0:T(8,128)S(1)}) fusion(f32[128]{0:T(128)S(1)} %get-tuple-element.76, bf16[3,128,1024]{2,1,0:T(8,128)(2,1)S(1)} %copy-done.18, s32[]{:T(128)S(6)} %min.34, bf16[1,1024,3072]{2,1,0:T(8,128)(2,1)} %param.11, bf16[128,2048]{1,0:T(8,128)(2,1)S(1)} %fusion.98, bf16[128,1024]{1,0:T(8,128)(2,1)S(1)} %copy-done.46), kind=kOutput, calls=%fused_computation.252 | convolution fusion | flops 807403392 | bytes 7865348 | tf_op jit(solution)/shard_map/nf,df->nd/dot_general | solution.py:365
  298.7 7.8 %collective-permute-done.23 = bf16[128,1024]{1,0:T(8,128)(2,1)S(1)} collective-permute-done((bf16[128,1024]{1,0:T(8,128)(2,1)S(1)}, bf16[128,1024]{1,0:T(8,128)(2,1)S(1)}, u32[]{:S(2)}, u32[]{:S(2)}) %collective-permute-start.23) | collective-permute-done | bytes 262176 | tf_op jit(solution)/shard_map/ppermute | solution.py:223
  310.7 3.4 convolution_bitcast_fusion
  314.1 3.9 fusion
  318.0 4.2 fusion.31
  322.2 2.9 reshape.446
  325.2 2.9 copy.69
  328.1 3.1 convolution_bitcast_fusion.1
  331.2 3.0 reshape.445
  334.1 2.9 copy.68
  337.1 4.9 %select_reduce_fusion.3 = (bf16[128,2048]{1,0:T(8,128)(2,1)}, bf16[128,2048]{1,0:T(8,128)(2,1)}, bf16[128,2048]{1,0:T(8,128)(2,1)}, bf16[128,2048]{1,0:T(8,128)(2,1)}) fusion(pred[3]{0:T(512)(128)(4,1)S(1)} %get-tuple-element.21, f32[4,128,1024]{2,1,0:T(8,128)} %copy.69, f32[4,128,1024]{2,1,0:T(8,128)} %copy.68, pred[3]{0:T(512)(128)(4,1)S(1)} %get-tuple-element.24, ...), kind=kLoop, calls=%fused_computation.41 | loop fusion | flops 6029312 | bytes 6291468 | tf_op jit(solution)/shard_map/reduce_sum | solution.py:361
  342.0 4.2 collective-permute-start.25
  354.0 6.3 %collective-permute-done.25 = bf16[128,2048]{1,0:T(8,128)(2,1)} collective-permute-done((bf16[128,2048]{1,0:T(8,128)(2,1)}, bf16[128,2048]{1,0:T(8,128)(2,1)}, u32[]{:S(2)}, u32[]{:S(2)}) %collective-permute-start.25) | collective-permute-done | bytes 524320 | tf_op jit(solution)/shard_map/ppermute | solution.py:217
  366.0 5.2 %fusion.162 = (f32[128]{0:T(128)S(1)}, f32[128,1024]{1,0:T(8,128)S(1)}) fusion(f32[128]{0:T(128)S(1)} %get-tuple-element.75, bf16[3,128,1024]{2,1,0:T(8,128)(2,1)S(1)} %copy-done.19, s32[]{:T(128)S(6)} %min.36, bf16[1,1024,3072]{2,1,0:T(8,128)(2,1)} %param.11, bf16[128,2048]{1,0:T(8,128)(2,1)S(1)} %fusion.93, bf16[128,1024]{1,0:T(8,128)(2,1)S(1)} %copy-done.48), kind=kOutput, calls=%fused_computation.244 | convolution fusion | flops 807403392 | bytes 7865348 | tf_op jit(solution)/shard_map/nf,df->nd/dot_general | solution.py:365
  372.1 51.5 %shard_map.93 = (f32[16,3072]{1,0:T(8,128)S(1)}, f32[16,1024]{1,0:T(8,128)S(1)}) custom-call(bf16[8,2,64,256]{3,2,1,0:T(8,128)(2,1)S(1)} %bitcast.457, bf16[8,2,64,256]{3,2,1,0:T(8,128)(2,1)S(1)} %bitcast.455, bf16[256,3072]{1,0:T(8,128)(2,1)S(1)} %bitcast.454, bf16[256,1024]{1,0:T(8,128)(2,1)S(1)} %bitcast.456), custom_call_target="tpu_custom_call" | custom-call | flops 2147483648 | bytes 4194304 | tf_op jit(solution)/shard_map/pallas_call | solution.py:181
  (310 shorter events, 133.7 us)
Async XLA Ops:
  0.6 18.4 %copy-start = (bf16[1,1024,1024]{2,1,0:T(8,128)(2,1)S(1)}, bf16[1,1024,1024]{2,1,0:T(8,128)(2,1)}, u32[]{:S(2)}) copy-start(bf16[1,1024,1024]{2,1,0:T(8,128)(2,1)} %param.12) | copy-start | bytes 6291460
  1.9 13.5 %copy-start.76 = (s32[2,1]{0,1:T(1,128)S(1)}, s32[2,1]{0,1:T(1,128)}, u32[]{:S(2)}) copy-start(s32[2,1]{0,1:T(1,128)} %param.10) | copy-start | bytes 28
  1.9 13.5 %copy-start.75 = (s32[2,1,3]{2,1,0:T(1,128)S(1)}, s32[2,1,3]{2,1,0:T(1,128)}, u32[]{:S(2)}) copy-start(s32[2,1,3]{2,1,0:T(1,128)} %param.9) | copy-start | bytes 76
  1.9 14.6 %copy-start.38 = (bf16[2,1,128,1024]{3,2,1,0:T(8,128)(2,1)S(1)}, bf16[2,1,128,1024]{3,2,1,0:T(8,128)(2,1)}, u32[]{:S(2)}) copy-start(bf16[2,1,128,1024]{3,2,1,0:T(8,128)(2,1)} %param.13) | copy-start | bytes 1572868
  7.7 29.9 %copy-start.21 = (bf16[1,128,2048]{2,1,0:T(8,128)(2,1)}, bf16[1,128,2048]{2,1,0:T(8,128)(2,1)S(1)}, u32[]{:S(2)}) copy-start(bf16[1,128,2048]{2,1,0:T(8,128)(2,1)S(1)} %get-tuple-element.73) | copy-start | bytes 1572868
  7.7 12.8 %collective-permute-start.2 = (bf16[128,2048]{1,0:T(8,128)(2,1)}, bf16[128,2048]{1,0:T(8,128)(2,1)}, u32[]{:S(2)}, u32[]{:S(2)}) collective-permute-start(bf16[128,2048]{1,0:T(8,128)(2,1)} %get-tuple-element.74), channel_id=1, source_target_pairs={{0,60},{4,0},{8,4},{12,8},{16,12},{20,16},{24,20},{28,24},{32,28},... | collective-permute-start | bytes 1572872 | tf_op jit(solution)/shard_map/ppermute | solution.py:217
  11.2 16.1 %collective-permute-start.1 = (bf16[128,2048]{1,0:T(8,128)(2,1)}, bf16[128,2048]{1,0:T(8,128)(2,1)}, u32[]{:S(2)}, u32[]{:S(2)}) collective-permute-start(bf16[128,2048]{1,0:T(8,128)(2,1)} %get-tuple-element.74), channel_id=1, source_target_pairs={{0,4},{4,8},{8,12},{12,16},{16,20},{20,24},{24,28},{28,32},{32,36}... | collective-permute-start | bytes 1572872 | tf_op jit(solution)/shard_map/ppermute | solution.py:217
  11.2 17.2 %collective-permute-start = (bf16[128,2048]{1,0:T(8,128)(2,1)}, bf16[128,2048]{1,0:T(8,128)(2,1)}, u32[]{:S(2)}, u32[]{:S(2)}) collective-permute-start(bf16[128,2048]{1,0:T(8,128)(2,1)} %get-tuple-element.74), channel_id=1, source_target_pairs={{0,8},{4,12},{8,16},{12,20},{16,24},{20,28},{24,32},{28,36},{32,40... | collective-permute-start | bytes 1572872 | tf_op jit(solution)/shard_map/ppermute | solution.py:217
  11.2 18.2 %collective-permute-start.3 = (bf16[128,2048]{1,0:T(8,128)(2,1)}, bf16[128,2048]{1,0:T(8,128)(2,1)}, u32[]{:S(2)}, u32[]{:S(2)}) collective-permute-start(bf16[128,2048]{1,0:T(8,128)(2,1)} %get-tuple-element.74), channel_id=1, source_target_pairs={{0,56},{4,60},{8,0},{12,4},{16,8},{20,12},{24,16},{28,20},{32,24},... | collective-permute-start | bytes 1572872 | tf_op jit(solution)/shard_map/ppermute | solution.py:217
  48.8 12.7 %copy-start.53 = (bf16[128,1024]{1,0:T(8,128)(2,1)}, bf16[128,1024]{1,0:T(8,128)(2,1)S(1)}, u32[]{:S(2)}) copy-start(bf16[128,1024]{1,0:T(8,128)(2,1)S(1)} %fusion.77) | copy-start | bytes 786436
  48.8 8.5 %collective-permute-start.4 = (bf16[128,1024]{1,0:T(8,128)(2,1)S(1)}, bf16[128,1024]{1,0:T(8,128)(2,1)}, u32[]{:S(2)}, u32[]{:S(2)}) collective-permute-start(bf16[128,1024]{1,0:T(8,128)(2,1)S(1)} %fusion.77), channel_id=1, source_target_pairs={{0,64},{1,65},{2,66},{3,67},{4,68},{5,69},{6,70},{7,71},{8,72},{9,... | collective-permute-start | bytes 786440 | tf_op jit(solution)/shard_map/ppermute | solution.py:223
  57.5 12.2 %copy-start.49 = (f32[8,128,512]{2,1,0:T(8,128)S(1)}, f32[8,128,512]{2,1,0:T(8,128)}, u32[]{:S(2)}) copy-start(f32[8,128,512]{2,1,0:T(8,128)} %get-tuple-element.95) | copy-start | bytes 6291460
  62.3 10.5 %collective-permute-start.7 = (bf16[128,2048]{1,0:T(8,128)(2,1)S(1)}, bf16[128,2048]{1,0:T(8,128)(2,1)S(1)}, u32[]{:S(2)}, u32[]{:S(2)}) collective-permute-start(bf16[128,2048]{1,0:T(8,128)(2,1)S(1)} %get-tuple-element.72), channel_id=1, source_target_pairs={{0,60},{4,0},{8,4},{12,8},{16,12},{20,16},{24,20},{28,24},{32,28},... | collective-permute-start | bytes 1572872 | tf_op jit(solution)/shard_map/ppermute | solution.py:217
  65.0 15.5 %collective-permute-start.6 = (bf16[128,2048]{1,0:T(8,128)(2,1)S(1)}, bf16[128,2048]{1,0:T(8,128)(2,1)S(1)}, u32[]{:S(2)}, u32[]{:S(2)}) collective-permute-start(bf16[128,2048]{1,0:T(8,128)(2,1)S(1)} %get-tuple-element.72), channel_id=1, source_target_pairs={{0,4},{4,8},{8,12},{12,16},{16,20},{20,24},{24,28},{28,32},{32,36}... | collective-permute-start | bytes 1572872 | tf_op jit(solution)/shard_map/ppermute | solution.py:217
  65.3 16.9 %collective-permute-start.5 = (bf16[128,2048]{1,0:T(8,128)(2,1)S(1)}, bf16[128,2048]{1,0:T(8,128)(2,1)S(1)}, u32[]{:S(2)}, u32[]{:S(2)}) collective-permute-start(bf16[128,2048]{1,0:T(8,128)(2,1)S(1)} %get-tuple-element.72), channel_id=1, source_target_pairs={{0,8},{4,12},{8,16},{12,20},{16,24},{20,28},{24,32},{28,36},{32,40... | collective-permute-start | bytes 1572872 | tf_op jit(solution)/shard_map/ppermute | solution.py:217
  67.0 18.4 %collective-permute-start.8 = (bf16[128,2048]{1,0:T(8,128)(2,1)S(1)}, bf16[128,2048]{1,0:T(8,128)(2,1)S(1)}, u32[]{:S(2)}, u32[]{:S(2)}) collective-permute-start(bf16[128,2048]{1,0:T(8,128)(2,1)S(1)} %get-tuple-element.72), channel_id=1, source_target_pairs={{0,56},{4,60},{8,0},{12,4},{16,8},{20,12},{24,16},{28,20},{32,24},... | collective-permute-start | bytes 1572872 | tf_op jit(solution)/shard_map/ppermute | solution.py:217
  104.1 13.0 %slice-start = ((s8[6291456]{0:T(1024)(128)(4,1)}), s8[4194304]{0:T(1024)(128)(4,1)S(1)}, s32[]{:S(2)}) async-start(s8[6291456]{0:T(1024)(128)(4,1)} %bitcast.460), calls=%async_computation | async-start | bytes 8388608
  104.6 9.4 %copy-start.67 = (bf16[128,1024]{1,0:T(8,128)(2,1)}, bf16[128,1024]{1,0:T(8,128)(2,1)S(1)}, u32[]{:S(2)}) copy-start(bf16[128,1024]{1,0:T(8,128)(2,1)S(1)} %fusion.74) | copy-start | bytes 786436
  104.6 12.5 %slice-start.1 = ((s8[6291456]{0:T(1024)(128)(4,1)}), s8[2097152]{0:T(1024)(128)(4,1)S(1)}, s32[]{:S(2)}) async-start(s8[6291456]{0:T(1024)(128)(4,1)} %bitcast.460), calls=%async_computation.1 | async-start | bytes 4194304
  104.6 12.1 %collective-permute-start.9 = (bf16[128,1024]{1,0:T(8,128)(2,1)S(1)}, bf16[128,1024]{1,0:T(8,128)(2,1)S(1)}, u32[]{:S(2)}, u32[]{:S(2)}) collective-permute-start(bf16[128,1024]{1,0:T(8,128)(2,1)S(1)} %fusion.74), channel_id=1, source_target_pairs={{0,64},{1,65},{2,66},{3,67},{4,68},{5,69},{6,70},{7,71},{8,72},{9,... | collective-permute-start | bytes 786440 | tf_op jit(solution)/shard_map/ppermute | solution.py:223
  118.2 9.0 %copy-start.57 = (bf16[1,128,1024]{2,1,0:T(8,128)(2,1)S(1)}, bf16[1,128,1024]{2,1,0:T(8,128)(2,1)}, u32[]{:S(2)}) copy-start(bf16[1,128,1024]{2,1,0:T(8,128)(2,1)} %fusion.199) | copy-start | bytes 786436
  120.1 18.8 %collective-permute-start.12 = (bf16[128,2048]{1,0:T(8,128)(2,1)}, bf16[128,2048]{1,0:T(8,128)(2,1)}, u32[]{:S(2)}, u32[]{:S(2)}) collective-permute-start(bf16[128,2048]{1,0:T(8,128)(2,1)} %get-tuple-element.70), channel_id=1, source_target_pairs={{0,60},{4,0},{8,4},{12,8},{16,12},{20,16},{24,20},{28,24},{32,28},... | collective-permute-start | bytes 1572872 | tf_op jit(solution)/shard_map/ppermute | solution.py:217
  121.1 17.8 %collective-permute-start.11 = (bf16[128,2048]{1,0:T(8,128)(2,1)}, bf16[128,2048]{1,0:T(8,128)(2,1)}, u32[]{:S(2)}, u32[]{:S(2)}) collective-permute-start(bf16[128,2048]{1,0:T(8,128)(2,1)} %get-tuple-element.70), channel_id=1, source_target_pairs={{0,4},{4,8},{8,12},{12,16},{16,20},{20,24},{24,28},{28,32},{32,36}... | collective-permute-start | bytes 1572872 | tf_op jit(solution)/shard_map/ppermute | solution.py:217
  121.7 17.2 %collective-permute-start.10 = (bf16[128,2048]{1,0:T(8,128)(2,1)}, bf16[128,2048]{1,0:T(8,128)(2,1)}, u32[]{:S(2)}, u32[]{:S(2)}) collective-permute-start(bf16[128,2048]{1,0:T(8,128)(2,1)} %get-tuple-element.70), channel_id=1, source_target_pairs={{0,8},{4,12},{8,16},{12,20},{16,24},{20,28},{24,32},{28,36},{32,40... | collective-permute-start | bytes 1572872 | tf_op jit(solution)/shard_map/ppermute | solution.py:217
  123.3 18.7 %collective-permute-start.13 = (bf16[128,2048]{1,0:T(8,128)(2,1)}, bf16[128,2048]{1,0:T(8,128)(2,1)}, u32[]{:S(2)}, u32[]{:S(2)}) collective-permute-start(bf16[128,2048]{1,0:T(8,128)(2,1)} %get-tuple-element.70), channel_id=1, source_target_pairs={{0,56},{4,60},{8,0},{12,4},{16,8},{20,12},{24,16},{28,20},{32,24},... | collective-permute-start | bytes 1572872 | tf_op jit(solution)/shard_map/ppermute | solution.py:217
  201.5 14.9 %collective-permute-start.14 = (bf16[128,2048]{1,0:T(8,128)(2,1)}, bf16[128,2048]{1,0:T(8,128)(2,1)}, u32[]{:S(2)}, u32[]{:S(2)}) collective-permute-start(bf16[128,2048]{1,0:T(8,128)(2,1)} %get-tuple-element.17), channel_id=1, source_target_pairs={{0,56},{4,60},{8,0},{12,4},{16,8},{20,12},{24,16},{28,20},{32,24},... | collective-permute-start | bytes 1572872 | tf_op jit(solution)/shard_map/ppermute | solution.py:217
  203.4 17.4 %collective-permute-start.15 = (bf16[128,2048]{1,0:T(8,128)(2,1)}, bf16[128,2048]{1,0:T(8,128)(2,1)}, u32[]{:S(2)}, u32[]{:S(2)}) collective-permute-start(bf16[128,2048]{1,0:T(8,128)(2,1)} %get-tuple-element.18), channel_id=1, source_target_pairs={{0,60},{4,0},{8,4},{12,8},{16,12},{20,16},{24,20},{28,24},{32,28},... | collective-permute-start | bytes 1572872 | tf_op jit(solution)/shard_map/ppermute | solution.py:217
  203.6 17.2 %collective-permute-start.16 = (bf16[128,2048]{1,0:T(8,128)(2,1)}, bf16[128,2048]{1,0:T(8,128)(2,1)}, u32[]{:S(2)}, u32[]{:S(2)}) collective-permute-start(bf16[128,2048]{1,0:T(8,128)(2,1)} %get-tuple-element.19), channel_id=1, source_target_pairs={{0,4},{4,8},{8,12},{12,16},{16,20},{20,24},{24,28},{28,32},{32,36}... | collective-permute-start | bytes 1572872 | tf_op jit(solution)/shard_map/ppermute | solution.py:217
  204.1 17.2 %collective-permute-start.17 = (bf16[128,2048]{1,0:T(8,128)(2,1)}, bf16[128,2048]{1,0:T(8,128)(2,1)}, u32[]{:S(2)}, u32[]{:S(2)}) collective-permute-start(bf16[128,2048]{1,0:T(8,128)(2,1)} %get-tuple-element.20), channel_id=1, source_target_pairs={{0,8},{4,12},{8,16},{12,20},{16,24},{20,28},{24,32},{28,36},{32,40... | collective-permute-start | bytes 1572872 | tf_op jit(solution)/shard_map/ppermute | solution.py:217
  207.0 16.4 %copy-start.44 = (bf16[128,1024]{1,0:T(8,128)(2,1)}, bf16[128,1024]{1,0:T(8,128)(2,1)S(1)}, u32[]{:S(2)}) copy-start(bf16[128,1024]{1,0:T(8,128)(2,1)S(1)} %copy.54) | copy-start | bytes 786436
  207.0 16.4 %slice-start.2 = ((s8[6291456]{0:T(1024)(128)(4,1)}), s8[4194304]{0:T(1024)(128)(4,1)S(1)}, s32[]{:S(2)}) async-start(s8[6291456]{0:T(1024)(128)(4,1)} %bitcast.462), calls=%async_computation.2 | async-start | bytes 8388608
  207.0 14.3 %copy-start.2 = (f32[4,128,1024]{2,1,0:T(8,128)S(1)}, f32[4,128,1024]{2,1,0:T(8,128)}, u32[]{:S(2)}) copy-start(f32[4,128,1024]{2,1,0:T(8,128)} %copy.53) | copy-start | bytes 6291460
  207.1 16.4 %slice-start.3 = ((s8[6291456]{0:T(1024)(128)(4,1)}), s8[2097152]{0:T(1024)(128)(4,1)S(1)}, s32[]{:S(2)}) async-start(s8[6291456]{0:T(1024)(128)(4,1)} %bitcast.462), calls=%async_computation.3 | async-start | bytes 4194304
  209.8 23.8 %copy-start.69 = (bf16[8,128,128]{2,1,0:T(8,128)(2,1)}, bf16[8,128,128]{2,1,0:T(8,128)(2,1)S(1)}, u32[]{:S(2)}) copy-start(bf16[8,128,128]{2,1,0:T(8,128)(2,1)S(1)} %convolution_convert_fusion.3) | copy-start | bytes 786436
  209.8 13.6 %copy-start.17 = (bf16[3,128,1024]{2,1,0:T(8,128)(2,1)S(1)}, bf16[3,128,1024]{2,1,0:T(8,128)(2,1)}, u32[]{:S(2)}) copy-start(bf16[3,128,1024]{2,1,0:T(8,128)(2,1)} %pad_maximum_fusion.13) | copy-start | bytes 2359300
  226.1 10.2 %collective-permute-start.18 = (bf16[128,1024]{1,0:T(8,128)(2,1)S(1)}, bf16[128,1024]{1,0:T(8,128)(2,1)S(1)}, u32[]{:S(2)}, u32[]{:S(2)}) collective-permute-start(bf16[128,1024]{1,0:T(8,128)(2,1)S(1)} %fusion.180), channel_id=1, source_target_pairs={{64,0},{65,1},{66,2},{67,3},{68,4},{69,5},{70,6},{71,7},{72,8},{73... | collective-permute-start | bytes 786440 | tf_op jit(solution)/shard_map/ppermute | solution.py:223
  262.1 10.5 %copy-start.54 = (bf16[128,1024]{1,0:T(8,128)(2,1)S(1)}, bf16[128,1024]{1,0:T(8,128)(2,1)}, u32[]{:S(2)}) copy-start(bf16[128,1024]{1,0:T(8,128)(2,1)} %copy-done.53) | copy-start | bytes 786436
  262.1 10.5 %copy-start.68 = (bf16[128,1024]{1,0:T(8,128)(2,1)S(1)}, bf16[128,1024]{1,0:T(8,128)(2,1)}, u32[]{:S(2)}) copy-start(bf16[128,1024]{1,0:T(8,128)(2,1)} %copy-done.67) | copy-start | bytes 786436
  262.1 10.5 %copy-start.71 = (bf16[1,128,1024]{2,1,0:T(8,128)(2,1)S(1)}, bf16[1,128,1024]{2,1,0:T(8,128)(2,1)}, u32[]{:S(2)}) copy-start(bf16[1,128,1024]{2,1,0:T(8,128)(2,1)} %fusion.80) | copy-start | bytes 786436
  262.1 11.6 %copy-start.52 = (bf16[8,128,128]{2,1,0:T(8,128)(2,1)S(1)}, bf16[8,128,128]{2,1,0:T(8,128)(2,1)}, u32[]{:S(2)}) copy-start(bf16[8,128,128]{2,1,0:T(8,128)(2,1)} %copy-done.51) | copy-start | bytes 786436
  262.1 11.6 %copy-start.66 = (bf16[8,128,128]{2,1,0:T(8,128)(2,1)S(1)}, bf16[8,128,128]{2,1,0:T(8,128)(2,1)}, u32[]{:S(2)}) copy-start(bf16[8,128,128]{2,1,0:T(8,128)(2,1)} %copy-done.65) | copy-start | bytes 786436
  262.1 11.6 %copy-start.70 = (bf16[8,128,128]{2,1,0:T(8,128)(2,1)S(1)}, bf16[8,128,128]{2,1,0:T(8,128)(2,1)}, u32[]{:S(2)}) copy-start(bf16[8,128,128]{2,1,0:T(8,128)(2,1)} %copy-done.69) | copy-start | bytes 786436
  267.0 12.4 %collective-permute-start.19 = (bf16[128,2048]{1,0:T(8,128)(2,1)}, bf16[128,2048]{1,0:T(8,128)(2,1)}, u32[]{:S(2)}, u32[]{:S(2)}) collective-permute-start(bf16[128,2048]{1,0:T(8,128)(2,1)} %get-tuple-element.13), channel_id=1, source_target_pairs={{0,56},{4,60},{8,0},{12,4},{16,8},{20,12},{24,16},{28,20},{32,24},... | collective-permute-start | bytes 1572872 | tf_op jit(solution)/shard_map/ppermute | solution.py:217
  267.0 18.3 %collective-permute-start.20 = (bf16[128,2048]{1,0:T(8,128)(2,1)}, bf16[128,2048]{1,0:T(8,128)(2,1)}, u32[]{:S(2)}, u32[]{:S(2)}) collective-permute-start(bf16[128,2048]{1,0:T(8,128)(2,1)} %get-tuple-element.14), channel_id=1, source_target_pairs={{0,60},{4,0},{8,4},{12,8},{16,12},{20,16},{24,20},{28,24},{32,28},... | collective-permute-start | bytes 1572872 | tf_op jit(solution)/shard_map/ppermute | solution.py:217
  271.4 16.1 %collective-permute-start.21 = (bf16[128,2048]{1,0:T(8,128)(2,1)}, bf16[128,2048]{1,0:T(8,128)(2,1)}, u32[]{:S(2)}, u32[]{:S(2)}) collective-permute-start(bf16[128,2048]{1,0:T(8,128)(2,1)} %get-tuple-element.15), channel_id=1, source_target_pairs={{0,4},{4,8},{8,12},{12,16},{16,20},{20,24},{24,28},{28,32},{32,36}... | collective-permute-start | bytes 1572872 | tf_op jit(solution)/shard_map/ppermute | solution.py:217
  271.4 17.2 %collective-permute-start.22 = (bf16[128,2048]{1,0:T(8,128)(2,1)}, bf16[128,2048]{1,0:T(8,128)(2,1)}, u32[]{:S(2)}, u32[]{:S(2)}) collective-permute-start(bf16[128,2048]{1,0:T(8,128)(2,1)} %get-tuple-element.16), channel_id=1, source_target_pairs={{0,8},{4,12},{8,16},{12,20},{16,24},{20,28},{24,32},{28,36},{32,40... | collective-permute-start | bytes 1572872 | tf_op jit(solution)/shard_map/ppermute | solution.py:217
  277.0 13.8 %copy-start.18 = (bf16[3,128,1024]{2,1,0:T(8,128)(2,1)S(1)}, bf16[3,128,1024]{2,1,0:T(8,128)(2,1)}, u32[]{:S(2)}) copy-start(bf16[3,128,1024]{2,1,0:T(8,128)(2,1)} %pad_maximum_fusion.13) | copy-start | bytes 2359300
  277.0 13.8 %copy-start.46 = (bf16[128,1024]{1,0:T(8,128)(2,1)S(1)}, bf16[128,1024]{1,0:T(8,128)(2,1)}, u32[]{:S(2)}) copy-start(bf16[128,1024]{1,0:T(8,128)(2,1)} %copy.62) | copy-start | bytes 786436
  296.2 10.4 %copy-start.40 = (bf16[2,1,128,1024]{3,2,1,0:T(8,128)(2,1)S(1)}, bf16[2,1,128,1024]{3,2,1,0:T(8,128)(2,1)}, u32[]{:S(2)}) copy-start(bf16[2,1,128,1024]{3,2,1,0:T(8,128)(2,1)} %param.13) | copy-start | bytes 1572868
  296.5 10.2 %copy-start.62 = (bf16[128,1024]{1,0:T(8,128)(2,1)}, bf16[128,1024]{1,0:T(8,128)(2,1)S(1)}, u32[]{:S(2)}) copy-start(bf16[128,1024]{1,0:T(8,128)(2,1)S(1)} %fusion.173) | copy-start | bytes 786436
  296.5 10.1 %collective-permute-start.23 = (bf16[128,1024]{1,0:T(8,128)(2,1)S(1)}, bf16[128,1024]{1,0:T(8,128)(2,1)S(1)}, u32[]{:S(2)}, u32[]{:S(2)}) collective-permute-start(bf16[128,1024]{1,0:T(8,128)(2,1)S(1)} %fusion.173), channel_id=1, source_target_pairs={{64,0},{65,1},{66,2},{67,3},{68,4},{69,5},{70,6},{71,7},{72,8},{73... | collective-permute-start | bytes 786440 | tf_op jit(solution)/shard_map/ppermute | solution.py:223
  337.1 10.9 %copy-start.28 = (bf16[128,2048]{1,0:T(8,128)(2,1)S(1)}, bf16[128,2048]{1,0:T(8,128)(2,1)}, u32[]{:S(2)}) copy-start(bf16[128,2048]{1,0:T(8,128)(2,1)} %copy-done.27) | copy-start | bytes 1572868
  337.1 10.9 %copy-start.47 = (bf16[128,1024]{1,0:T(8,128)(2,1)S(1)}, bf16[128,1024]{1,0:T(8,128)(2,1)}, u32[]{:S(2)}) copy-start(bf16[128,1024]{1,0:T(8,128)(2,1)} %copy.62) | copy-start | bytes 786436
  337.1 11.8 %copy-start.9 = (bf16[8,128,512]{2,1,0:T(8,128)(2,1)S(1)}, bf16[8,128,512]{2,1,0:T(8,128)(2,1)}, u32[]{:S(2)}) copy-start(bf16[8,128,512]{2,1,0:T(8,128)(2,1)} %fusion.31) | copy-start | bytes 3145732
  337.1 11.8 %copy-start.32 = (bf16[64,8,8,128]{3,2,1,0:T(8,128)(2,1)S(1)}, bf16[64,8,8,128]{3,2,1,0:T(8,128)(2,1)}, u32[]{:S(2)}) copy-start(bf16[64,8,8,128]{3,2,1,0:T(8,128)(2,1)} %copy.93) | copy-start | bytes 3145732
  342.0 12.0 %collective-permute-start.24 = (bf16[128,2048]{1,0:T(8,128)(2,1)}, bf16[128,2048]{1,0:T(8,128)(2,1)}, u32[]{:S(2)}, u32[]{:S(2)}) collective-permute-start(bf16[128,2048]{1,0:T(8,128)(2,1)} %get-tuple-element.9), channel_id=1, source_target_pairs={{0,56},{4,60},{8,0},{12,4},{16,8},{20,12},{24,16},{28,20},{32,24},... | collective-permute-start | bytes 1572872 | tf_op jit(solution)/shard_map/ppermute | solution.py:217
  342.0 18.3 %collective-permute-start.25 = (bf16[128,2048]{1,0:T(8,128)(2,1)}, bf16[128,2048]{1,0:T(8,128)(2,1)}, u32[]{:S(2)}, u32[]{:S(2)}) collective-permute-start(bf16[128,2048]{1,0:T(8,128)(2,1)} %get-tuple-element.10), channel_id=1, source_target_pairs={{0,60},{4,0},{8,4},{12,8},{16,12},{20,16},{24,20},{28,24},{32,28},... | collective-permute-start | bytes 1572872 | tf_op jit(solution)/shard_map/ppermute | solution.py:217
  346.2 15.9 %collective-permute-start.26 = (bf16[128,2048]{1,0:T(8,128)(2,1)}, bf16[128,2048]{1,0:T(8,128)(2,1)}, u32[]{:S(2)}, u32[]{:S(2)}) collective-permute-start(bf16[128,2048]{1,0:T(8,128)(2,1)} %get-tuple-element.11), channel_id=1, source_target_pairs={{0,4},{4,8},{8,12},{12,16},{16,20},{20,24},{24,28},{28,32},{32,36}... | collective-permute-start | bytes 1572872 | tf_op jit(solution)/shard_map/ppermute | solution.py:217
  346.2 17.4 %collective-permute-start.27 = (bf16[128,2048]{1,0:T(8,128)(2,1)}, bf16[128,2048]{1,0:T(8,128)(2,1)}, u32[]{:S(2)}, u32[]{:S(2)}) collective-permute-start(bf16[128,2048]{1,0:T(8,128)(2,1)} %get-tuple-element.12), channel_id=1, source_target_pairs={{0,8},{4,12},{8,16},{12,20},{16,24},{20,28},{24,32},{28,36},{32,40... | collective-permute-start | bytes 1572872 | tf_op jit(solution)/shard_map/ppermute | solution.py:217
  353.2 12.7 %copy-start.48 = (bf16[128,1024]{1,0:T(8,128)(2,1)S(1)}, bf16[128,1024]{1,0:T(8,128)(2,1)}, u32[]{:S(2)}) copy-start(bf16[128,1024]{1,0:T(8,128)(2,1)} %copy.70) | copy-start | bytes 786436
  353.2 12.7 %copy-start.19 = (bf16[3,128,1024]{2,1,0:T(8,128)(2,1)S(1)}, bf16[3,128,1024]{2,1,0:T(8,128)(2,1)}, u32[]{:S(2)}) copy-start(bf16[3,128,1024]{2,1,0:T(8,128)(2,1)} %pad_maximum_fusion.13) | copy-start | bytes 2359300
  372.0 51.6 %copy-start.31 = (bf16[128,1024]{1,0:T(8,128)(2,1)S(1)}, bf16[128,1024]{1,0:T(8,128)(2,1)}, u32[]{:S(2)}) copy-start(bf16[128,1024]{1,0:T(8,128)(2,1)} %copy-done.30) | copy-start | bytes 786436
  372.1 51.8 %copy-start.56 = (bf16[128,1024]{1,0:T(8,128)(2,1)S(1)}, bf16[128,1024]{1,0:T(8,128)(2,1)}, u32[]{:S(2)}) copy-start(bf16[128,1024]{1,0:T(8,128)(2,1)} %copy-done.55) | copy-start | bytes 786436
  372.1 51.8 %copy-start.63 = (bf16[128,1024]{1,0:T(8,128)(2,1)S(1)}, bf16[128,1024]{1,0:T(8,128)(2,1)}, u32[]{:S(2)}) copy-start(bf16[128,1024]{1,0:T(8,128)(2,1)} %copy-done.62) | copy-start | bytes 786436
  (45 other events, 186.0 us)

commit v2 on v1

v2 whole, which is shorter than its diff:
```python
import functools
import math

import jax
import jax.numpy as jnp
from jax import lax
from jax.experimental import pallas as pl
from jax.experimental.pallas import tpu as pltpu
from jax.sharding import PartitionSpec as P

HEAD_DIM = 128
EPSILON = 1e-06
NEGATIVE = -1e30
MESH = pl.DeviceIdType.MESH
CHUNK = 512
PAIRS = ((6, 7), (0, 1), (2, 3), (4, 5))


def wgrad_kernel(
    share, nT, aT, proj, og, gin, gout,
    nT_r, aT_r, proj_r, og_r, G, r1, r2, r3, r4, r5,
    xs, xr, ss, rs,
):
    view = lax.axis_index("view")
    zi = lax.axis_index("dp")
    core = lax.rem(view, 2)
    yi = lax.rem(view // 2, 4)
    xi = view // 8
    peer = xi * 8 + yi * 2 + (1 - core)
    across = (1 - xi) * 8 + yi * 2 + core

    def y_dev(step):
        return {"view": xi * 8 + lax.rem(yi + step + 4, 4) * 2 + core}

    def z_dev(step):
        return {"dp": lax.rem(zi + step + 4, 4)}

    barrier = pltpu.get_barrier_semaphore()
    partners = ({"view": peer}, {"view": across}, y_dev(1), y_dev(-1), z_dev(1), z_dev(-1))
    for dev in partners:
        pl.semaphore_signal(barrier, inc=1, device_id=dev, device_id_type=MESH)
    pl.semaphore_wait(barrier, len(partners))

    def remote(src, dst, s, r, dev):
        return pltpu.make_async_remote_copy(
            src_ref=src, dst_ref=dst, send_sem=s, recv_sem=r, device_id=dev, device_id_type=MESH
        )

    def cols(ref, k):
        return ref.at[:, pl.ds(k * CHUNK, CHUNK)]

    pieces = {}
    pieces["a"] = remote(aT.at[:, 1 - core], aT_r, xs.at[8], xr.at[8], {"view": peer})
    pieces["n"] = remote(nT.at[:, 1 - core], nT_r, xs.at[9], xr.at[9], {"view": peer})
    for n in range(6):
        pieces[n] = remote(cols(proj, n), cols(proj_r, n), xs.at[n], xr.at[n], {"view": peer})
    for n in range(6, 8):
        pieces[n] = remote(
            cols(og, n - 6), cols(og_r, n - 6), xs.at[n], xr.at[n], {"view": peer}
        )
    for key in ("a", 6, 7, "n", 0, 1, 2, 3, 4, 5):
        pieces[key].start()

    def first(n, x_at, a):
        return G.at[n, x_at, a] if n % 2 == 0 else G.at[n, x_at, :, a]

    def second(n, x_at, a, b):
        return G.at[n, x_at, a, b] if n % 2 == 0 else G.at[n, x_at, b, a]

    whole = slice(None)
    sent = []

    def send(n, k, src, dst, dev):
        copy = remote(src, dst, ss.at[n, k], rs.at[n, k], dev)
        copy.start()
        sent.append(copy)
        return copy

    arrived = {}

    def add_into(ref, *others):
        total = ref[...].astype(jnp.float32)
        for other in others:
            total = total + other[...].astype(jnp.float32)
        ref[...] = total.astype(jnp.bfloat16)

    seen = set()

    def need(key):
        if key not in seen:
            seen.add(key)
            pieces[key].wait_recv()

    def stage(n, s):
        a, b = (yi, zi) if n % 2 == 0 else (zi, yi)
        dev1, dev2 = (y_dev, z_dev) if n % 2 == 0 else (z_dev, y_dev)
        if s == 0:
            if n >= 6:
                need("a")
                left, left_r, right, right_r, k = aT, aT_r, og, og_r, n - 6
            else:
                need("n")
                left, left_r, right, right_r, k = nT, nT_r, proj, proj_r, n
            need(n)
            rows = left.shape[0] * left.shape[2]
            toks = left.shape[3]
            mine = left[:, core].reshape(rows, toks)
            theirs = left_r[...].reshape(rows, toks)
            part = jnp.dot(
                mine, right[:, k * CHUNK : (k + 1) * CHUNK], preferred_element_type=jnp.float32
            ) + jnp.dot(
                theirs, right_r[:, k * CHUNK : (k + 1) * CHUNK], preferred_element_type=jnp.float32
            )
            G[n] = part.astype(jnp.bfloat16).reshape(G.shape[1:])
            opp = lax.rem(a + 2, 4)
            arrived[n, 0] = (
                send(n, 0, first(n, 0, opp), r1.at[n, 0], dev1(1)),
                send(n, 1, first(n, 1, opp), r1.at[n, 1], dev1(-1)),
            )
            return
        for copy in arrived[n, s - 1]:
            copy.wait_recv()
        if s == 1:
            up, down = lax.rem(a + 1, 4), lax.rem(a + 3, 4)
            add_into(first(n, 0, up), r1.at[n, 0])
            add_into(first(n, 1, down), r1.at[n, 1])
            arrived[n, 1] = (
                send(n, 2, first(n, whole, up), r2.at[n, 0], dev1(1)),
                send(n, 3, first(n, whole, down), r2.at[n, 1], dev1(-1)),
            )
        elif s == 2:
            add_into(first(n, whole, a), r2.at[n, 0], r2.at[n, 1])
            opp = lax.rem(b + 2, 4)
            arrived[n, 2] = (
                send(n, 4, second(n, 0, a, opp), r3.at[n, 0], dev2(1)),
                send(n, 5, second(n, 1, a, opp), r3.at[n, 1], dev2(-1)),
            )
        elif s == 3:
            up, down = lax.rem(b + 1, 4), lax.rem(b + 3, 4)
            add_into(second(n, 0, a, up), r3.at[n, 0])
            add_into(second(n, 1, a, down), r3.at[n, 1])
            arrived[n, 3] = (
                send(n, 6, second(n, whole, a, up), r4.at[n, 0], dev2(1)),
                send(n, 7, second(n, whole, a, down), r4.at[n, 1], dev2(-1)),
            )
        elif s == 4:
            add_into(second(n, whole, a, b), r4.at[n, 0], r4.at[n, 1])
            arrived[n, 4] = (
                send(n, 8, second(n, 1 - xi, a, b), r5.at[n], {"view": across}),
            )
        else:
            total = second(n, xi, a, b)[...].astype(jnp.float32) + r5[n].astype(jnp.float32)
            out, k = (gin, n) if n < 6 else (gout, n - 6)
            out[:, k * CHUNK : (k + 1) * CHUNK] = total * share

    stages = 6
    for turn in range(len(PAIRS) + stages - 1):
        for p in range(len(PAIRS)):
            s = turn - p
            if 0 <= s < stages:
                for n in PAIRS[p]:
                    stage(n, s)
    for copy in list(pieces.values()) + sent:
        copy.wait_send()


def weight_grads(nT, aT, proj, outgrad, share):
    toks, width = outgrad.shape
    chunks = 4 * width // CHUNK
    rows = width // 64
    vm = pl.BlockSpec(memory_space=pltpu.VMEM)
    bf = jnp.bfloat16
    return pl.pallas_call(
        functools.partial(wgrad_kernel, share),
        out_shape=(
            jax.ShapeDtypeStruct((rows, 3 * width), jnp.float32),
            jax.ShapeDtypeStruct((rows, width), jnp.float32),
        ),
        in_specs=[vm] * 4,
        out_specs=(vm, vm),
        scratch_shapes=[
            pltpu.VMEM((8, width // 16, toks), bf),
            pltpu.VMEM((8, width // 16, toks), bf),
            pltpu.VMEM((toks, 3 * width), bf),
            pltpu.VMEM((toks, width), bf),
            pltpu.VMEM((chunks, 2, 4, 4, rows, CHUNK), bf),
            pltpu.VMEM((chunks, 2, 4, rows, CHUNK), bf),
            pltpu.VMEM((chunks, 2, 2, 4, rows, CHUNK), bf),
            pltpu.VMEM((chunks, 2, rows, CHUNK), bf),
            pltpu.VMEM((chunks, 2, 2, rows, CHUNK), bf),
            pltpu.VMEM((chunks, rows, CHUNK), bf),
            pltpu.SemaphoreType.DMA((10,)),
            pltpu.SemaphoreType.DMA((10,)),
            pltpu.SemaphoreType.DMA((chunks, 9)),
            pltpu.SemaphoreType.DMA((chunks, 9)),
        ],
        compiler_params=pltpu.CompilerParams(
            collective_id=1, has_side_effects=True, vmem_limit_bytes=40 * 1024 * 1024
        ),
        cost_estimate=pl.CostEstimate(
            flops=2 * 512 * 512 * 4096, bytes_accessed=4 << 20, transcendentals=0
        ),
    )(nT, aT, proj, outgrad)


def ticks_kernel(
    scale,
    x_ref, cot_ref, live_ref, win_hbm, wout_hbm,
    out_ref, grad_ref, nT_ref, aT_ref, proj_ref, og_ref,
    win, wout, X, N, Q, KV, PR, AT, FA, AG, OWN, SP, RP,
    wsem, s_x, r_x, s_hop, r_hop, s_p, r_p,
):
    sec = lax.axis_index("section")
    view = lax.axis_index("view")
    views = lax.axis_size("view")
    core = lax.rem(view, 2)
    peer = {"view": view + 1 - 2 * core}
    ahead = {"view": lax.rem(view + 2, views)}
    behind = {"view": lax.rem(view + views - 2, views)}
    other = {"section": 1 - sec}
    micros, toks, width = x_ref.shape
    heads = width // HEAD_DIM
    relay = 3 - core
    straight = 2 + core
    tile = 512
    f32, bf = jnp.float32, jnp.bfloat16

    loads = [
        pltpu.make_async_copy(win_hbm, win, wsem.at[0]),
        pltpu.make_async_copy(wout_hbm, wout, wsem.at[1]),
    ]
    for load in loads:
        load.start()

    barrier = pltpu.get_barrier_semaphore()
    for dev in (peer, ahead, behind, other):
        pl.semaphore_signal(barrier, inc=1, device_id=dev, device_id_type=MESH)
    pl.semaphore_wait(barrier, 4)

    def remote(src, dst, s, r, dev):
        return pltpu.make_async_remote_copy(
            src_ref=src, dst_ref=dst, send_sem=s, recv_sem=r, device_id=dev, device_id_type=MESH
        )

    def spread(m):
        return [
            remote(X.at[m, 0], X.at[m, 1], s_x.at[m, 0], r_x.at[m, 0], peer),
            remote(X.at[m, 0], X.at[m, 2], s_x.at[m, 1], r_x.at[m, 1], ahead),
            remote(X.at[m, 0], X.at[m, 3], s_x.at[m, 2], r_x.at[m, 2], behind),
        ]

    def pass_on(m):
        return remote(X.at[m, relay], X.at[m, 4], s_x.at[m, 3], r_x.at[m, 3], peer)

    def hop_out(m):
        return remote(out_ref.at[m], X.at[m, 0], s_hop.at[m], r_hop.at[m], other)

    def hop_back(m):
        return remote(grad_ref.at[m], og_ref.at[m], s_hop.at[m], r_hop.at[m], other)

    def parts(m):
        return {
            "diag": remote(SP.at[m, 3], RP.at[m, 3], s_p.at[m, 3], r_p.at[m, 3], peer),
            "peer": remote(SP.at[m, 0], RP.at[m, 0], s_p.at[m, 0], r_p.at[m, 0], peer),
            "behind": remote(SP.at[m, 1], RP.at[m, 1], s_p.at[m, 1], r_p.at[m, 1], behind),
            "ahead": remote(SP.at[m, 2], RP.at[m, 2], s_p.at[m, 2], r_p.at[m, 2], ahead),
        }

    def start_spread(m):
        for copy in spread(m):
            copy.start()

    @pl.when(sec == 0)
    def _():
        for m in range(micros):
            X[m, 0] = x_ref[m]
            start_spread(m)

    @pl.when(sec == 1)
    def _():
        for m in range(micros):
            og_ref[m] = cot_ref[m]

    def norm_block(m, k):
        rows = X[m, k].astype(f32)
        factor = lax.rsqrt(jnp.mean(rows * rows, -1, keepdims=True) + EPSILON)
        normed = (rows * factor).astype(bf)
        N[k] = normed
        return factor, normed

    def project(m, k0, k1):
        rows = (k1 - k0) * toks
        left = N.at[pl.ds(k0, k1 - k0)]

        @pl.loop(0, 2 * width // tile)
        def _(j):
            at = pl.multiple_of(j * tile, tile)
            block = jnp.dot(
                left[...].reshape(rows, width),
                win[:, pl.ds(width + at, tile)],
                preferred_element_type=f32,
            ).astype(bf)
            KV[m, k0 * toks : k1 * toks, pl.ds(at, tile)] = block

    def forward(m):
        @pl.when(sec == 1)
        def _():
            if m == 0:
                hop_out(m).wait_recv()
                start_spread(m)

        copies = spread(m)
        factor, normed = norm_block(m, 0)
        FA[m] = factor
        nT_ref[:, :, :, m * toks : (m + 1) * toks] = normed.T.reshape(
            8, 2, width // 16, toks
        )
        if m == 0:
            loads[0].wait()

        @pl.loop(0, width // tile)
        def _(j):
            at = pl.multiple_of(j * tile, tile)
            Q[m, :, pl.ds(at, tile)] = jnp.dot(
                N[0], win[:, pl.ds(at, tile)], preferred_element_type=f32
            ).astype(bf)

        copies[0].wait_recv()
        norm_block(m, 1)
        project(m, 0, 2)
        copies[1].wait_recv()
        copies[2].wait_recv()
        pass_on(m).start()
        norm_block(m, 2)
        norm_block(m, 3)
        project(m, 2, 4)
        pass_on(m).wait_recv()
        norm_block(m, 4)
        project(m, 4, 5)
        if m == 0:
            @pl.when(sec == 1)
            def _():
                hop_out(1).wait_recv()
                start_spread(1)

        live = live_ref[m] > 0.0

        def head(h, carry):
            at = pl.multiple_of(h * HEAD_DIM, HEAD_DIM)
            cols = pl.ds(at, HEAD_DIM)
            scores = lax.dot_general(
                Q[m, :, cols], KV[m, :, cols], (((1,), (1,)), ((), ())),
                preferred_element_type=f32,
            ) * scale
            masked = jnp.where(live, scores, NEGATIVE)
            terms = jnp.exp(masked - jnp.max(masked, -1, keepdims=True))
            prob = terms * (1.0 / jnp.sum(terms, -1, keepdims=True))
            PR[m, h] = prob
            AT[m, :, cols] = jnp.dot(
                prob.astype(bf), KV[m, :, pl.ds(width + at, HEAD_DIM)],
                preferred_element_type=f32,
            ).astype(bf)
            return carry

        lax.fori_loop(0, heads, head, 0, unroll=2)
        if m == 0:
            loads[1].wait()

        @pl.loop(0, width // tile)
        def _(j):
            cols = pl.ds(pl.multiple_of(j * tile, tile), tile)
            branch = jnp.dot(AT[m], wout[:, cols], preferred_element_type=f32)
            out_ref[m, :, cols] = (X[m, 0, :, cols].astype(f32) + branch).astype(bf)

        @pl.when(sec == 0)
        def _():
            hop_out(m).start()

        aT_ref[:, :, :, m * toks : (m + 1) * toks] = AT[m].T.reshape(8, 2, width // 16, toks)

    def backward(m):
        @pl.when(sec == 0)
        def _():
            hop_back(m).wait_recv()

        @pl.loop(0, width // tile)
        def _(j):
            at = pl.multiple_of(j * tile, tile)
            AG[:, pl.ds(at, tile)] = lax.dot_general(
                og_ref[m], wout[pl.ds(at, tile)], (((1,), (1,)), ((), ())),
                preferred_element_type=f32,
            ).astype(bf)

        def head(h, carry):
            at = pl.multiple_of(h * HEAD_DIM, HEAD_DIM)
            cols = pl.ds(at, HEAD_DIM)
            vcols = pl.ds(width + at, HEAD_DIM)
            gh = AG[:, cols]
            prob = PR[m, h]
            prob_grad = lax.dot_general(
                gh, KV[m, :, vcols], (((1,), (1,)), ((), ())), preferred_element_type=f32
            )
            row_dot = jnp.sum(prob * prob_grad, -1, keepdims=True)
            score_grad = (prob * (prob_grad - row_dot) * scale).astype(bf)
            proj_ref[m, :, cols] = jnp.dot(
                score_grad, KV[m, :, cols], preferred_element_type=f32
            ).astype(bf)
            key_part = lax.dot_general(
                score_grad, Q[m, :, cols], (((0,), (0,)), ((), ())), preferred_element_type=f32
            )
            value_part = lax.dot_general(
                prob.astype(bf), gh, (((0,), (0,)), ((), ())), preferred_element_type=f32
            )
            OWN[m, :, cols] = key_part[:toks]
            OWN[m, :, vcols] = value_part[:toks]
            for k in range(4):
                SP[m, k, :, cols] = key_part[(k + 1) * toks : (k + 2) * toks].astype(bf)
                SP[m, k, :, vcols] = value_part[(k + 1) * toks : (k + 2) * toks].astype(bf)
            return carry

        lax.fori_loop(0, heads, head, 0, unroll=2)
        copies = parts(m)
        copies["diag"].start()

        @pl.when(core == 0)
        def _():
            copies["behind"].start()

        @pl.when(core == 1)
        def _():
            copies["ahead"].start()

        copies["peer"].start()
        copies["diag"].wait_recv()
        SP[m, relay - 1] = (
            SP[m, relay - 1].astype(f32) + RP[m, 3].astype(f32)
        ).astype(bf)

        @pl.when(core == 0)
        def _():
            copies["ahead"].start()

        @pl.when(core == 1)
        def _():
            copies["behind"].start()

    def finish(m):
        copies = parts(m)
        for name in ("peer", "behind", "ahead"):
            copies[name].wait_recv()
        total = OWN[m]
        for k in range(3):
            total = total + RP[m, k].astype(f32)
        proj_ref[m, :, width:] = total.astype(bf)

        @pl.loop(0, width // tile)
        def _(j):
            at = pl.multiple_of(j * tile, tile)
            OWN[m, :, pl.ds(at, tile)] = lax.dot_general(
                proj_ref[m], win[pl.ds(at, tile)], (((1,), (1,)), ((), ())),
                preferred_element_type=f32,
            )

        normed_grad = OWN[m, :, :width]
        factor = FA[m]
        unit = X[m, 0].astype(f32) * factor
        inner = jnp.mean(normed_grad * unit, -1, keepdims=True)
        grad_ref[m] = (
            og_ref[m].astype(f32) + factor * (normed_grad - unit * inner)
        ).astype(bf)

        @pl.when(sec == 1)
        def _():
            hop_back(m).start()

    for m in range(micros):
        forward(m)
    for m in range(micros):
        backward(m)
    for m in range(micros):
        finish(m)

    for m in range(micros):
        for copy in spread(m) + [pass_on(m)] + list(parts(m).values()):
            copy.wait_send()

        @pl.when(sec == 0)
        def _():
            hop_out(m).wait_send()

        @pl.when(sec == 1)
        def _():
            hop_back(m).wait_send()


def run_ticks(x, cot, live, w_in, w_out):
    micros, toks, width = x.shape
    heads = width // HEAD_DIM
    blocks = 5
    vm = pl.BlockSpec(memory_space=pltpu.VMEM)
    hbm = pl.BlockSpec(memory_space=pl.ANY)
    bf, f32 = jnp.bfloat16, jnp.float32
    sds = jax.ShapeDtypeStruct
    dma = pltpu.SemaphoreType.DMA
    return pl.pallas_call(
        functools.partial(ticks_kernel, 1.0 / math.sqrt(HEAD_DIM)),
        out_shape=(
            sds((micros, toks, width), bf),
            sds((micros, toks, width), bf),
            sds((8, 2, width // 16, micros * toks), bf),
            sds((8, 2, width // 16, micros * toks), bf),
            sds((micros, toks, 3 * width), bf),
            sds((micros, toks, width), bf),
        ),
        in_specs=[vm, vm, vm, hbm, hbm],
        out_specs=(vm,) * 6,
        scratch_shapes=[
            pltpu.VMEM((width, 3 * width), bf),
            pltpu.VMEM((width, width), bf),
            pltpu.VMEM((micros, blocks, toks, width), bf),
            pltpu.VMEM((blocks, toks, width), bf),
            pltpu.VMEM((micros, toks, width), bf),
            pltpu.VMEM((micros, blocks * toks, 2 * width), bf),
            pltpu.VMEM((micros, heads, toks, blocks * toks), f32),
            pltpu.VMEM((micros, toks, width), bf),
            pltpu.VMEM((micros, toks, 1), f32),
            pltpu.VMEM((toks, width), bf),
            pltpu.VMEM((micros, toks, 2 * width), f32),
            pltpu.VMEM((micros, 4, toks, 2 * width), bf),
            pltpu.VMEM((micros, 4, toks, 2 * width), bf),
            dma((2,)),
            dma((micros, 4)), dma((micros, 4)),
            dma((micros,)), dma((micros,)),
            dma((micros, 4)), dma((micros, 4)),
        ],
        compiler_params=pltpu.CompilerParams(
            collective_id=2, has_side_effects=True, vmem_limit_bytes=56 * 1024 * 1024
        ),
        cost_estimate=pl.CostEstimate(
            flops=20 * 10**9, bytes_accessed=12 << 20, transcendentals=2 * 10**6
        ),
    )(x, cot, live, w_in, w_out)


def on_device(scenes, neighbours, counts, w_in, w_out, cotangent):
    views = lax.axis_size("view")
    micros, _, toks, width = scenes.shape
    slots = neighbours.shape[2]
    view = lax.axis_index("view")
    core = view % 2
    side = 1 - 2 * core
    offsets = jnp.stack([0 * core, side, -2 + 0 * core, 2 + 0 * core, -side])
    slot_live = jnp.arange(slots, dtype=jnp.int32)[None, :] < counts
    rel = (neighbours[:, 0, :] - view) % views
    hit = (rel[:, :, None] == (offsets % views)[None, None, :]) & slot_live[:, :, None]
    block_live = jnp.any(hit, 1).at[:, 0].set(True)
    live = jnp.repeat(block_live.astype(jnp.float32), toks, axis=1)[:, None, :]
    share = 1.0 / (micros * lax.axis_size("dp"))
    outputs, grads, nT, aT, proj, outgrad = run_ticks(
        scenes[:, 0], cotangent[:, 0], live, w_in[0], w_out[0]
    )
    grad_in, grad_out = weight_grads(
        nT, aT, proj.reshape(-1, 3 * width), outgrad.reshape(-1, width), share
    )
    return (outputs[None, :, None], grads[None, :, None], grad_in[None], grad_out[None])


def solution(mesh):
    in_specs = (
        P("dp", "view", None, None),
        P("dp", "view", None),
        P("dp", "view"),
        P("section", None, None),
        P("section", None, None),
        P("dp", "view", None, None),
    )
    out_specs = (
        P("section", "dp", "view", None, None),
        P("section", "dp", "view", None, None),
        P("section", ("view", "dp"), None),
        P("section", ("view", "dp"), None),
    )
    return jax.shard_map(
        on_device, mesh=mesh, in_specs=in_specs, out_specs=out_specs, check_vma=False
    )
```

time: 435 us -> 186 us (0.43); the launches traced: 427 us -> 186 us
  Pallas kernels: 51.5 us -> 174 us
  local copies, waits for them, and re-layouts: 103 us -> 8.24 us
  matrix products: 84.5 us -> 0 us
  waiting for transfers between devices: 72.2 us -> 0 us
  other arithmetic: 62.5 us -> 2.82 us
  starting transfers between devices: 51.1 us -> 0 us
    pallas_call x0 -> x1, Pallas kernels: none -> 126 us  [run_ticks(): pl.pallas_call(functools.partial(ticks_kernel, 1.0 / math.sqrt(HEAD_DIM))...]
    ppermute x28 -> x0, waiting for transfers between devices: 72.2 us -> none  [the longest x24 58.1 us: from_behind(): return lax.ppermute(value, axis, pairs)]
    dot_general x27 -> x0, matrix products: 62.5 us -> none  [the longest x3 12.7 us: on_device(): jnp.einsum('nf,df->nd', proj_grad, weight_in, preferred_element_type=jnp....]
    ppermute x28 -> x0, starting transfers between devices: 51.1 us -> none  [the longest x24 36.2 us: from_behind(): return lax.ppermute(value, axis, pairs)]
    reshape x15 -> x0, local copies, waits for them, and re-layouts: 37.2 us -> none  [the longest x6 17.6 us: on_device(): key_part.reshape(block_total, token_rows, model_width)]
    another operation x22 -> x2, other arithmetic: 28.1 us -> 1.29 us  [the longest x4 7.86 us: on_device(): prob_stack = jnp.stack(prob_list)]
    unnamed x176 -> x16, local copies, waits for them, and re-layouts: 29.7 us -> 7.43 us
    sub x6 -> x0, matrix products: 22 us -> none  [the longest x3 11.6 us: on_device(): prob_grad - row_dot]
  transfers between devices with their start and end apart: 28 -> 0, of which waited for: 22 -> 0; matrix products, arithmetic and copies ran while one was open for 11% -> 0% of each run, Pallas kernels for 0% -> 0%
where the time goes in v2:
time: 186 us
  Pallas kernels  174 us (94%)
  local copies, waits for them, and re-layouts  8.24 us (4%)
  other arithmetic  2.82 us (2%)
    pallas_call x1, Pallas kernels, run_ticks(): pl.pallas_call(functools.partial(ticks_kernel, 1.0 / math.sqrt(HEAD_DIM))...  126 us
    pallas_call x1, Pallas kernels, weight_grads(): pl.pallas_call(functools.partial(wgrad_kernel, share), out_shape=(jax.Sha...  48.1 us
    unnamed x16, local copies, waits for them, and re-layouts  7.43 us

profile of v2, /device:TPU:0, one launch (start us, length us, event | category | flops | bytes accessed | tf_op | source)
XLA Modules:
  0.0 185.9 jit_solution(12446916484551361100)
XLA Ops:
  0.6 0.1 stack.11
  0.7 0.7 broadcast_subtract_fusion
  1.4 0.7 iota_compare_fusion
  2.2 0.1 and_reduce_fusion
  2.3 0.6 compare_reduce_fusion
  2.9 0.7 slice_select_fusion
  3.6 0.1 broadcast_in_dim.19
  3.7 0.6 broadcast_in_dim_reshape.4.live_ref
  4.3 126.0 %shard_map.96 = (bf16[2,128,1024]{2,1,0:T(8,128)(2,1)}, bf16[2,128,1024]{2,1,0:T(8,128)(2,1)}, bf16[8,2,64,256]{3,2,1,0:T(8,128)(2,1)}, bf16[8,2,64,256]{3,2,1,0...) custom-call(bf16[2,128,1024]{2,1,0:T(8,128)(2,1)} %bitcast.27, ...), custom_call_target="tpu_custom_call" | custom-call | flops 20000000000 | bytes 12582912 | tf_op jit(solution)/shard_map/pallas_call | solution.py:505
  130.3 0.0 copy-start
  130.3 1.4 copy-done
  131.7 0.0 copy-start.1
  131.7 1.0 copy-done.1
  132.8 0.0 copy-start.2
  132.8 1.0 copy-done.2
  133.8 0.0 copy-start.3
  133.8 1.0 copy-done.3
  134.8 0.0 copy-start.5
  134.8 0.0 copy-start.4
  134.8 48.1 %shard_map.97 = (f32[16,3072]{1,0:T(8,128)S(1)}, f32[16,1024]{1,0:T(8,128)S(1)}) custom-call(bf16[8,2,64,256]{3,2,1,0:T(8,128)(2,1)S(1)} %copy-done.2, bf16[8,2,64,256]{3,2,1,0:T(8,128)(2,1)S(1)} %copy-done.3, bf16[256,3072]{1,0:T(8,128)(2,1)S(1)} %bitcast.20, bf16[256,1024]{1,0:T(8,128)(2,1)S(1)} %bitcast.21), custom_call_target="tpu_custom_call" | custom-call | flops 2147483648 | bytes 4194304 | tf_op jit(solution)/shard_map/pallas_call | solution.py:173
  183.0 0.0 copy-done.5
  183.0 0.8 copy.23
  183.8 0.0 copy-done.4
  183.8 0.8 copy.24
  184.6 0.7 copy.25
  185.3 0.6 copy.26
  (4 shorter events, 0.1 us)
Async XLA Ops:
  130.3 1.4 copy-start
  131.7 1.0 copy-start.1
  132.8 1.0 copy-start.2
  133.8 1.0 copy-start.3
  134.8 48.1 %copy-start.5 = (bf16[2,128,1024]{2,1,0:T(8,128)(2,1)S(1)}, bf16[2,128,1024]{2,1,0:T(8,128)(2,1)}, u32[]{:S(2)}) copy-start(bf16[2,128,1024]{2,1,0:T(8,128)(2,1)} %get-tuple-element.24) | copy-start | bytes 1572868
  134.8 49.0 %copy-start.4 = (bf16[2,128,1024]{2,1,0:T(8,128)(2,1)S(1)}, bf16[2,128,1024]{2,1,0:T(8,128)(2,1)}, u32[]{:S(2)}) copy-start(bf16[2,128,1024]{2,1,0:T(8,128)(2,1)} %get-tuple-element.25) | copy-start | bytes 1572868

commit v3 on v0

v3 whole, which is shorter than its diff:
```python
import functools
import math

import jax
import jax.numpy as jnp
from jax import lax
from jax.experimental import pallas as pl
from jax.experimental.pallas import tpu as pltpu
from jax.sharding import PartitionSpec as P

HEAD_DIM = 128
EPSILON = 1e-06
NEGATIVE = -1e30
MESH = pl.DeviceIdType.MESH
CHUNK = 512
PAIRS = ((6, 7), (0, 1), (2, 3), (4, 5))
STAGES = 6
PIECES = 4
BLOCKS = 5
LAST = (((1,), (1,)), ((), ()))


def scene_kernel(
    scale, share,
    x_ref, cot_ref, nbr_ref, cnt_ref, win_hbm, wout_hbm,
    out_ref, grad_ref, gin, gout,
    win, wout, X, OG, N, QKV, AG, PR, AT, FA, ST, SS, RD, NG,
    LN, LA, SN, SA, RP, RO, G, r1, r2, r3, r4, r5,
    wsem, s_sp, r_sp, s_h, r_h, s_q, r_q, s_a, r_a, s_st, r_st, s_rd, r_rd,
    s_l, r_l, s_o, r_o, s_pj, r_pj, ss, rs,
):
    sec = lax.axis_index("section")
    view = lax.axis_index("view")
    zi = lax.axis_index("dp")
    core = lax.rem(view, 2)
    yi = lax.rem(view // 2, 4)
    xi = view // 8
    micros, toks, width = x_ref.shape
    heads = width // HEAD_DIM
    relay = 3 - core
    f32, bf = jnp.float32, jnp.bfloat16

    peer = {"view": view + 1 - 2 * core}
    ahead = {"view": lax.rem(view + 2, 16)}
    behind = {"view": lax.rem(view + 14, 16)}
    diag = {"view": lax.rem(view + 15 + 2 * core, 16)}
    other = {"section": 1 - sec}
    across = {"view": lax.rem(view + 8, 16)}

    def y_dev(step):
        return {"view": xi * 8 + lax.rem(yi + step + 4, 4) * 2 + core}

    def z_dev(step):
        return {"dp": lax.rem(zi + step + 4, 4)}

    loads = [
        pltpu.make_async_copy(win_hbm, win, wsem.at[0]),
        pltpu.make_async_copy(wout_hbm, wout, wsem.at[1]),
    ]
    for load in loads:
        load.start()

    partners = (
        peer, ahead, behind, diag, other, across, y_dev(1), y_dev(-1), z_dev(1), z_dev(-1)
    )
    barrier = pltpu.get_barrier_semaphore()
    for dev in partners:
        pl.semaphore_signal(barrier, inc=1, device_id=dev, device_id_type=MESH)
    pl.semaphore_wait(barrier, len(partners))

    def remote(src, dst, s, r, dev):
        return pltpu.make_async_remote_copy(
            src_ref=src, dst_ref=dst, send_sem=s, recv_sem=r, device_id=dev, device_id_type=MESH
        )

    def when_section(s):
        return pl.when(sec == s)

    step = toks // PIECES

    def spread(t, m, way, i):
        buf = (X, OG)[t]
        rows = pl.ds(i * step, step)
        return remote(
            buf.at[m, 0, rows], buf.at[m, 1 + way, rows],
            s_sp.at[t, m, way, i], r_sp.at[t, m, way, i], (ahead, behind)[way],
        )

    def hop(t, m, i):
        src, dst = ((out_ref, X), (grad_ref, OG))[t]
        rows = pl.ds(i * step, step)
        return remote(
            src.at[m, rows], dst.at[m, 0, rows], s_h.at[m, i], r_h.at[m, i], other
        )

    def share_qkv(m, which, j):
        src, dst = ((0, 1), (relay, 4))[which]
        cols = pl.ds(j * width, width)
        return remote(
            QKV.at[m, src, :, cols], QKV.at[m, dst, :, cols],
            s_q.at[m, which, j], r_q.at[m, which, j], peer,
        )

    def share_ag(m, which):
        src, dst = ((0, 1), (relay, 4))[which]
        return remote(AG.at[m, src], AG.at[m, dst], s_a.at[m, which], r_a.at[m, which], peer)

    ROUTES = {1: (1, peer), 3: (2, behind), 2: (3, ahead), 4: (4, diag)}

    def stats_to(m, block):
        target, dev = ROUTES[block]
        return remote(
            SS.at[m, target - 1], ST.at[m, block],
            s_st.at[m, block - 1], r_st.at[m, block - 1], dev,
        )

    def dots_to(m, block):
        return remote(
            RD.at[m, 0], RD.at[m, block],
            s_rd.at[m, block - 1], r_rd.at[m, block - 1], ROUTES[block][1],
        )

    own_toks = micros * toks

    def share_left(which):
        src, dst = ((SN, LN), (SA, LA))[which]
        return remote(
            src, dst.at[:, :, pl.ds(own_toks, own_toks)], s_l.at[which], r_l.at[which], peer
        )

    def share_og(m):
        return remote(RO.at[m], RO.at[micros + m], s_o.at[m], r_o.at[m], peer)

    def share_proj(m, which):
        cols = (pl.ds(0, width), pl.ds(width, 2 * width))[which]
        return remote(
            RP.at[m, :, cols], RP.at[micros + m, :, cols],
            s_pj.at[m, which], r_pj.at[m, which], peer,
        )

    def start_spread(t, m):
        for i in range(PIECES):
            spread(t, m, 0, i).start()
            spread(t, m, 1, i).start()

    def wait_spread(t, m):
        for i in range(PIECES):
            spread(t, m, 0, i).wait_recv()
            spread(t, m, 1, i).wait_recv()

    def receive_hop(t, m):
        for i in range(PIECES):
            hop(t, m, i).wait_recv()
            spread(t, m, 0, i).start()
            spread(t, m, 1, i).start()

    side = 1 - 2 * core
    offsets = (0, side, -2, 2, -side)

    def live_block(m, k):
        if k == 0:
            return jnp.ones((1, toks), f32)
        live = jnp.float32(0.0)
        for j in range(nbr_ref.shape[1]):
            rel = lax.rem(nbr_ref[m, j] - view - offsets[k] + 32, 16)
            hit = jnp.logical_and(rel == 0, j < cnt_ref[m, 0])
            live = jnp.where(hit, jnp.float32(1.0), live)
        return jnp.full((1, toks), live, f32)

    def norm_block(m, at):
        rows = X[m, at].astype(f32)
        factor = lax.rsqrt(jnp.mean(rows * rows, -1, keepdims=True) + EPSILON)
        normed = (rows * factor).astype(bf)
        N[at] = normed
        return factor, normed

    def keep_left(value, mine, theirs, m):
        parts = value.T.reshape(8, 2, width // 16, toks)
        cols = slice(m * toks, (m + 1) * toks)
        first, second = parts[:, 0], parts[:, 1]
        mine[:, :, cols] = jnp.where(core == 0, first, second)
        theirs[:, :, cols] = jnp.where(core == 0, second, first)

    def lanes():
        return lax.broadcasted_iota(jnp.int32, (toks, HEAD_DIM), 1)

    def forward(m):
        if m == 0:
            @when_section(1)
            def _():
                receive_hop(0, 0)

        factor, normed = norm_block(m, 0)
        FA[m] = factor
        for j in (1, 2, 0):
            cols = slice(j * width, (j + 1) * width)
            QKV[m, 0, :, cols] = jnp.dot(
                N[0], win[:, cols], preferred_element_type=f32
            ).astype(bf)
            share_qkv(m, 0, j).start()
        keep_left(normed, LN, SN, m)
        wait_spread(0, m)
        if m == 0:
            @when_section(0)
            def _():
                start_spread(0, 1)

        norm_block(m, 1)
        norm_block(m, 2)
        for j in (1, 2, 0):
            cols = slice(j * width, (j + 1) * width)
            near = jnp.dot(
                N[1:3].reshape(2 * toks, width), win[:, cols], preferred_element_type=f32
            ).astype(bf)
            QKV[m, 2:4, :, cols] = near.reshape(2, toks, width)
            share_qkv(m, 1, j).start()
        for j in (1, 2):
            share_qkv(m, 0, j).wait_recv()
            share_qkv(m, 1, j).wait_recv()
        lives = [live_block(m, k) for k in range(BLOCKS)]
        live = jnp.concatenate(lives, 1) > 0.0
        stats = jnp.zeros((toks, HEAD_DIM), f32)
        for h in range(heads):
            cols = slice(h * HEAD_DIM, (h + 1) * HEAD_DIM)
            kcols = slice(width + h * HEAD_DIM, width + (h + 1) * HEAD_DIM)
            vcols = slice(2 * width + h * HEAD_DIM, 2 * width + (h + 1) * HEAD_DIM)
            scores = lax.dot_general(
                QKV[m, 0, :, cols], QKV[m, :, :, kcols].reshape(BLOCKS * toks, HEAD_DIM), LAST,
                preferred_element_type=f32,
            ) * scale
            masked = jnp.where(live, scores, NEGATIVE)
            top = jnp.max(masked, -1, keepdims=True)
            terms = jnp.exp(masked - top)
            inverse = 1.0 / jnp.sum(terms, -1, keepdims=True)
            prob = terms * inverse
            PR[m, h] = prob
            AT[m, :, cols] = jnp.dot(
                prob.astype(bf), QKV[m, :, :, vcols].reshape(BLOCKS * toks, HEAD_DIM),
                preferred_element_type=f32,
            ).astype(bf)
            stats = jnp.where(lanes() == h, top, stats)
            stats = jnp.where(lanes() == heads + h, inverse, stats)
        if m == 0:
            @when_section(1)
            def _():
                receive_hop(0, 1)

            @when_section(0)
            def _():
                loads[1].wait()

        branch = jnp.dot(AT[m], wout[...], preferred_element_type=f32)
        out_ref[m] = (X[m, 0].astype(f32) + branch).astype(bf)

        @when_section(0)
        def _():
            for i in range(PIECES):
                hop(0, m, i).start()

        turned = stats.T
        ST[m, 0] = turned[: 2 * heads]
        for k in range(1, BLOCKS):
            SS[m, k - 1, :heads] = jnp.where(lives[k] > 0.0, turned[:heads], -NEGATIVE)
            SS[m, k - 1, heads:] = turned[heads : 2 * heads]
        for block in ROUTES:
            stats_to(m, block).start()
        keep_left(AT[m], LA, SA, m)

    def own_ag(m):
        AG[m, 0] = lax.dot_general(
            OG[m, 0], wout[...], LAST, preferred_element_type=f32
        ).astype(bf)
        share_ag(m, 0).start()

    def near_ag(m):
        wait_spread(1, m)
        near = lax.dot_general(
            OG[m, 1:3].reshape(2 * toks, width), wout[...], LAST, preferred_element_type=f32
        ).astype(bf)
        AG[m, 2:4] = near.reshape(2, toks, width)
        share_ag(m, 1).start()

    def backward(m):
        @when_section(0)
        def _():
            receive_hop(1, m)
            own_ag(m)

        RO[m] = OG[m, 0]
        share_og(m).start()
        dots = jnp.zeros((toks, HEAD_DIM), f32)
        for h in range(heads):
            cols = slice(h * HEAD_DIM, (h + 1) * HEAD_DIM)
            kcols = slice(width + h * HEAD_DIM, width + (h + 1) * HEAD_DIM)
            vcols = slice(2 * width + h * HEAD_DIM, 2 * width + (h + 1) * HEAD_DIM)
            prob = PR[m, h]
            prob_grad = lax.dot_general(
                AG[m, 0, :, cols], QKV[m, :, :, vcols].reshape(BLOCKS * toks, HEAD_DIM), LAST,
                preferred_element_type=f32,
            )
            row_dot = jnp.sum(prob * prob_grad, -1, keepdims=True)
            score_grad = (prob * (prob_grad - row_dot) * scale).astype(bf)
            RP[m, :, cols] = jnp.dot(
                score_grad, QKV[m, :, :, kcols].reshape(BLOCKS * toks, HEAD_DIM),
                preferred_element_type=f32,
            ).astype(bf)
            dots = jnp.where(lanes() == h, row_dot, dots)
        RD[m, 0] = dots.T[:heads]
        for block in ROUTES:
            dots_to(m, block).start()
        share_proj(m, 0).start()

        @when_section(0)
        def _():
            near_ag(m)

        for which in range(2):
            share_qkv(m, which, 0).wait_recv()
            share_ag(m, which).wait_recv()
        for block in ROUTES:
            stats_to(m, block).wait_recv()
            dots_to(m, block).wait_recv()

        def row(ref, h):
            return jnp.concatenate([ref[m, k, h : h + 1, :] for k in range(BLOCKS)], 1)

        for h in range(heads):
            cols = slice(h * HEAD_DIM, (h + 1) * HEAD_DIM)
            kcols = slice(width + h * HEAD_DIM, width + (h + 1) * HEAD_DIM)
            vcols = slice(2 * width + h * HEAD_DIM, 2 * width + (h + 1) * HEAD_DIM)
            queries = QKV[m, :, :, cols].reshape(BLOCKS * toks, HEAD_DIM)
            out_grads = AG[m, :, :, cols].reshape(BLOCKS * toks, HEAD_DIM)
            scores = lax.dot_general(
                QKV[m, 0, :, kcols], queries, LAST, preferred_element_type=f32
            ) * scale
            prob = jnp.exp(scores - row(ST, h)) * row(ST, heads + h)
            prob_grad = lax.dot_general(
                QKV[m, 0, :, vcols], out_grads, LAST, preferred_element_type=f32
            )
            score_grad = (prob * (prob_grad - row(RD, h)) * scale).astype(bf)
            RP[m, :, kcols] = jnp.dot(
                score_grad, queries, preferred_element_type=f32
            ).astype(bf)
            RP[m, :, vcols] = jnp.dot(
                prob.astype(bf), out_grads, preferred_element_type=f32
            ).astype(bf)
        share_proj(m, 1).start()

    def finish(m):
        half = width // 2
        for j in range(2):
            NG[:, j * half : (j + 1) * half] = lax.dot_general(
                RP[m], win[j * half : (j + 1) * half, :], LAST, preferred_element_type=f32
            )
        normed_grad = NG[...]
        factor = FA[m]
        unit = X[m, 0].astype(f32) * factor
        inner = jnp.mean(normed_grad * unit, -1, keepdims=True)
        grad_ref[m] = (
            OG[m, 0].astype(f32) + factor * (normed_grad - unit * inner)
        ).astype(bf)

    whole = slice(None)

    def first(n, x_at, a):
        return G.at[n, x_at, a] if n % 2 == 0 else G.at[n, x_at, :, a]

    def second(n, x_at, a, b):
        return G.at[n, x_at, a, b] if n % 2 == 0 else G.at[n, x_at, b, a]

    def ring(n, s):
        a, b = (yi, zi) if n % 2 == 0 else (zi, yi)
        dev1, dev2 = (y_dev, z_dev) if n % 2 == 0 else (z_dev, y_dev)

        def make(k, src, dst, dev):
            return remote(src, dst, ss.at[n, k], rs.at[n, k], dev)

        def turn(value, by):
            return lax.rem(value + by, 4)

        if s == 0:
            return (
                make(0, first(n, 0, turn(a, 2)), r1.at[n, 0], dev1(1)),
                make(1, first(n, 1, turn(a, 2)), r1.at[n, 1], dev1(-1)),
            )
        if s == 1:
            return (
                make(2, first(n, whole, turn(a, 1)), r2.at[n, 0], dev1(1)),
                make(3, first(n, whole, turn(a, 3)), r2.at[n, 1], dev1(-1)),
            )
        if s == 2:
            return (
                make(4, second(n, 0, a, turn(b, 2)), r3.at[n, 0], dev2(1)),
                make(5, second(n, 1, a, turn(b, 2)), r3.at[n, 1], dev2(-1)),
            )
        if s == 3:
            return (
                make(6, second(n, whole, a, turn(b, 1)), r4.at[n, 0], dev2(1)),
                make(7, second(n, whole, a, turn(b, 3)), r4.at[n, 1], dev2(-1)),
            )
        return (make(8, second(n, 1 - xi, a, b), r5.at[n], across),)

    def add_into(ref, *others):
        total = ref[...].astype(f32)
        for item in others:
            total = total + item[...].astype(f32)
        ref[...] = total.astype(bf)

    def stage(n, s):
        a, b = (yi, zi) if n % 2 == 0 else (zi, yi)
        if s > 0:
            for copy in ring(n, s - 1):
                copy.wait_recv()
        if s == 0:
            left = LA if n >= 6 else LN
            right, k = (RO, n - 6) if n >= 6 else (RP, n)
            part = jnp.dot(
                left[...].reshape(left.shape[0] * left.shape[1], 2 * own_toks),
                right[:, :, k * CHUNK : (k + 1) * CHUNK].reshape(2 * own_toks, CHUNK),
                preferred_element_type=f32,
            )
            G[n] = part.astype(bf).reshape(G.shape[1:])
        elif s == 1:
            add_into(first(n, 0, lax.rem(a + 1, 4)), r1.at[n, 0])
            add_into(first(n, 1, lax.rem(a + 3, 4)), r1.at[n, 1])
        elif s == 2:
            add_into(first(n, whole, a), r2.at[n, 0], r2.at[n, 1])
        elif s == 3:
            add_into(second(n, 0, a, lax.rem(b + 1, 4)), r3.at[n, 0])
            add_into(second(n, 1, a, lax.rem(b + 3, 4)), r3.at[n, 1])
        elif s == 4:
            add_into(second(n, whole, a, b), r4.at[n, 0], r4.at[n, 1])
        else:
            total = second(n, xi, a, b)[...].astype(f32) + r5[n].astype(f32)
            out, k = (gin, n) if n < 6 else (gout, n - 6)
            out[:, k * CHUNK : (k + 1) * CHUNK] = total * share
        if s < STAGES - 1:
            for copy in ring(n, s):
                copy.start()

    @when_section(0)
    def _():
        for m in range(micros):
            X[m, 0] = x_ref[m]
        start_spread(0, 0)

    @when_section(1)
    def _():
        for m in range(micros):
            OG[m, 0] = cot_ref[m]
            start_spread(1, m)

    loads[0].wait()

    @when_section(1)
    def _():
        loads[1].wait()
        for m in range(micros):
            own_ag(m)
            near_ag(m)

    for m in range(micros):
        forward(m)
    for which in range(2):
        share_left(which).start()
    for m in range(micros):
        backward(m)

        @when_section(1)
        def _():
            finish(m)
            for i in range(PIECES):
                hop(1, m, i).start()

    for m in range(micros):
        share_og(m).wait_recv()
    share_left(1).wait_recv()
    for turn in range(len(PAIRS) + STAGES - 1):
        for p in range(len(PAIRS)):
            s = turn - p
            if p == 1 and s == 0:
                share_left(0).wait_recv()
                for m in range(micros):
                    share_proj(m, 0).wait_recv()
            if p == 2 and s == 0:
                for m in range(micros):
                    share_proj(m, 1).wait_recv()
            if 0 <= s < STAGES:
                for n in PAIRS[p]:
                    stage(n, s)
        if turn in (2, 3):
            @when_section(0)
            def _():
                finish(turn - 2)

    for m in range(micros):
        for t in range(2):
            for i in range(PIECES):
                spread(t, m, 0, i).wait_send()
                spread(t, m, 1, i).wait_send()
        for i in range(PIECES):
            @when_section(0)
            def _():
                hop(0, m, i).wait_send()

            @when_section(1)
            def _():
                hop(1, m, i).wait_send()
        for which in range(2):
            for j in range(3):
                share_qkv(m, which, j).wait_send()
            share_ag(m, which).wait_send()
            share_proj(m, which).wait_send()
        for block in ROUTES:
            stats_to(m, block).wait_send()
            dots_to(m, block).wait_send()
        share_og(m).wait_send()
    for which in range(2):
        share_left(which).wait_send()
    for pair in PAIRS:
        for n in pair:
            for s in range(STAGES - 1):
                for copy in ring(n, s):
                    copy.wait_send()


def on_device(scenes, neighbours, counts, w_in, w_out, cotangent):
    micros, _, toks, width = scenes.shape
    heads = width // HEAD_DIM
    share = 1.0 / (micros * lax.axis_size("dp"))
    chunks = 4 * width // CHUNK
    rows = width // 64
    group = width // 16
    vm = pl.BlockSpec(memory_space=pltpu.VMEM)
    sm = pl.BlockSpec(memory_space=pltpu.SMEM)
    hbm = pl.BlockSpec(memory_space=pl.ANY)
    bf, f32 = jnp.bfloat16, jnp.float32
    sds = jax.ShapeDtypeStruct
    dma = pltpu.SemaphoreType.DMA
    outputs, grads, grad_in, grad_out = pl.pallas_call(
        functools.partial(scene_kernel, 1.0 / math.sqrt(HEAD_DIM), share),
        out_shape=(
            sds((micros, toks, width), bf),
            sds((micros, toks, width), bf),
            sds((rows, 3 * width), f32),
            sds((rows, width), f32),
        ),
        in_specs=[vm, vm, sm, sm, hbm, hbm],
        out_specs=(vm,) * 4,
        scratch_shapes=[
            pltpu.VMEM((width, 3 * width), bf),
            pltpu.VMEM((width, width), bf),
            pltpu.VMEM((micros, 3, toks, width), bf),
            pltpu.VMEM((micros, 3, toks, width), bf),
            pltpu.VMEM((3, toks, width), bf),
            pltpu.VMEM((micros, BLOCKS, toks, 3 * width), bf),
            pltpu.VMEM((micros, BLOCKS, toks, width), bf),
            pltpu.VMEM((micros, heads, toks, BLOCKS * toks), f32),
            pltpu.VMEM((micros, toks, width), bf),
            pltpu.VMEM((micros, toks, 1), f32),
            pltpu.VMEM((micros, BLOCKS, 2 * heads, toks), f32),
            pltpu.VMEM((micros, BLOCKS - 1, 2 * heads, toks), f32),
            pltpu.VMEM((micros, BLOCKS, heads, toks), f32),
            pltpu.VMEM((toks, width), f32),
            pltpu.VMEM((8, group, 2 * micros * toks), bf),
            pltpu.VMEM((8, group, 2 * micros * toks), bf),
            pltpu.VMEM((8, group, micros * toks), bf),
            pltpu.VMEM((8, group, micros * toks), bf),
            pltpu.VMEM((2 * micros, toks, 3 * width), bf),
            pltpu.VMEM((2 * micros, toks, width), bf),
            pltpu.VMEM((chunks, 2, 4, 4, rows, CHUNK), bf),
            pltpu.VMEM((chunks, 2, 4, rows, CHUNK), bf),
            pltpu.VMEM((chunks, 2, 2, 4, rows, CHUNK), bf),
            pltpu.VMEM((chunks, 2, rows, CHUNK), bf),
            pltpu.VMEM((chunks, 2, 2, rows, CHUNK), bf),
            pltpu.VMEM((chunks, rows, CHUNK), bf),
            dma((2,)),
            dma((2, micros, 2, PIECES)), dma((2, micros, 2, PIECES)),
            dma((micros, PIECES)), dma((micros, PIECES)),
            dma((micros, 2, 3)), dma((micros, 2, 3)),
            dma((micros, 2)), dma((micros, 2)),
            dma((micros, 4)), dma((micros, 4)),
            dma((micros, 4)), dma((micros, 4)),
            dma((2,)), dma((2,)),
            dma((micros,)), dma((micros,)),
            dma((micros, 2)), dma((micros, 2)),
            dma((chunks, 9)), dma((chunks, 9)),
        ],
        compiler_params=pltpu.CompilerParams(
            collective_id=1, has_side_effects=True, vmem_limit_bytes=60 * 1024 * 1024
        ),
        cost_estimate=pl.CostEstimate(
            flops=20 * 10**9, bytes_accessed=12 << 20, transcendentals=2 * 10**6
        ),
    )(scenes[:, 0], cotangent[:, 0], neighbours[:, 0], counts, w_in[0], w_out[0])
    return (outputs[None, :, None], grads[None, :, None], grad_in[None], grad_out[None])


def solution(mesh):
    in_specs = (
        P("dp", "view", None, None),
        P("dp", "view", None),
        P("dp", "view"),
        P("section", None, None),
        P("section", None, None),
        P("dp", "view", None, None),
    )
    out_specs = (
        P("section", "dp", "view", None, None),
        P("section", "dp", "view", None, None),
        P("section", ("view", "dp"), None),
        P("section", ("view", "dp"), None),
    )
    return jax.shard_map(
        on_device, mesh=mesh, in_specs=in_specs, out_specs=out_specs, check_vma=False
    )
```

time: 930 us -> 152 us (0.16)
  waiting for transfers between devices: 606 us -> 0 us
  Pallas kernels: 0 us -> 143 us
  matrix products: 94.1 us -> 0 us
  local copies, waits for them, and re-layouts: 96.8 us -> 8.12 us
  other arithmetic: 58.7 us -> 0 us
  starting transfers between devices: 50.4 us -> 0 us
  between operations: 15.6 us -> 0.64 us
    reduce_scatter x2 -> x0, waiting for transfers between devices: 517 us -> none  [the longest x1 305 us: on_device(): lax.psum_scatter(grad_in, ('view', 'dp'), scatter_dimension=0, tiled=True)]
    pallas_call x0 -> x1, Pallas kernels: none -> 143 us  [on_device(): pl.pallas_call(functools.partial(scene_kernel, 1.0 / math.sqrt(HEAD_DIM),...]
    ppermute x28 -> x0, waiting for transfers between devices: 88.4 us -> none  [the longest x24 70 us: from_behind(): return lax.ppermute(value, axis, pairs)]
    dot_general x29 -> x0, matrix products: 72.9 us -> none  [the longest x3 15.7 us: on_device(): jnp.einsum('nf,df->nd', proj_grad, weight_in, preferred_element_type=jnp....]
    ppermute x28 -> x0, starting transfers between devices: 50.3 us -> none  [the longest x24 35.5 us: from_behind(): return lax.ppermute(value, axis, pairs)]
    reshape x15 -> x0, local copies, waits for them, and re-layouts: 40.4 us -> none  [the longest x6 17.5 us: on_device(): key_part.reshape(block_total, token_rows, model_width)]
    another operation x19 -> x0, other arithmetic: 23.9 us -> none  [the longest x3 7.83 us: on_device(): candidates = jnp.stack(fetched)]
    sub x6 -> x0, matrix products: 21.2 us -> none  [the longest x3 10.9 us: on_device(): prob_grad - row_dot]
  transfers between devices with their start and end apart: 30 -> 0, of which waited for: 27 -> 0; matrix products, arithmetic and copies ran while one was open for 10% -> 0% of each run, Pallas kernels for 0% -> 0%
where the time goes in v3:
time: 152 us
  Pallas kernels  143 us (94%)
  local copies, waits for them, and re-layouts  8.12 us (5%)
    pallas_call x1, Pallas kernels, on_device(): pl.pallas_call(functools.partial(scene_kernel, 1.0 / math.sqrt(HEAD_DIM),...  143 us
    unnamed x5, local copies, waits for them, and re-layouts  8.12 us

profile of v3, /device:TPU:0, one launch (start us, length us, event | category | flops | bytes accessed | tf_op | source)
XLA Modules:
  0.0 151.9 jit_solution(15105138951585471357)
XLA Ops:
  0.6 1.3 copy.10.cnt_ref
  1.9 143.1 %shard_map.93 = (bf16[2,128,1024]{2,1,0:T(8,128)(2,1)}, bf16[2,128,1024]{2,1,0:T(8,128)(2,1)}, f32[16,3072]{1,0:T(8,128)}, f32[16,1024]{1,0:T(8,128)}) custom-call(bf16[2,128,1024]{2,1,0:T(8,128)(2,1)} %bitcast.19, bf16[2,128,1024]{2,1,0:T(8,128)(2,1)} %bitcast.20, s32[2,3]{1,0:T(2,128)} %bitcast.21, s32[2,1]{1,0:T(2,128)} %copy.10.cnt_ref, ...), custom_call_target="tpu_custom_call" | custom-call | flops 20000000000 | bytes 12582912 | tf_op jit(solution)/shard_map/pallas_call | solution.py:540
  145.1 1.9 %copy.17 = bf16[1,2,1,128,1024]{4,3,2,1,0:T(8,128)(2,1)} copy(bf16[1,2,1,128,1024]{4,3,2,1,0:T(8,128)(2,1)} %bitcast.14) | data formatting | bytes 1048576
  147.0 1.9 %copy.18 = bf16[1,2,1,128,1024]{4,3,2,1,0:T(8,128)(2,1)} copy(bf16[1,2,1,128,1024]{4,3,2,1,0:T(8,128)(2,1)} %bitcast.13) | data formatting | bytes 1048576
  148.8 1.6 %copy.19 = f32[1,16,3072]{2,1,0:T(8,128)} copy(f32[1,16,3072]{2,1,0:T(8,128)} %bitcast.15) | data formatting | bytes 393216
  150.4 1.5 copy.20

commit v4 on v3

v4 whole, which is shorter than its diff:
```python
import functools
import math

import jax
import jax.numpy as jnp
from jax import lax
from jax.experimental import pallas as pl
from jax.experimental.pallas import tpu as pltpu
from jax.sharding import PartitionSpec as P

HEAD_DIM = 128
EPSILON = 1e-06
NEGATIVE = -1e30
MESH = pl.DeviceIdType.MESH
CHUNK = 512
PAIRS = ((6, 7), (0, 1), (2, 4), (3, 5))
FAR = tuple((dx, db) for dx in range(2) for db in range(4) if dx or db)
PIECES = 4
BLOCKS = 5
LAST = (((1,), (1,)), ((), ()))


def scene_kernel(
    scale, share,
    x_hbm, cot_hbm, nbr_ref, cnt_ref, win_hbm, wout_hbm,
    out_hbm, grad_hbm, gin_hbm, gout_hbm,
    out_ref, grad_ref, gin, gout, win, winT, wout, X, OG, N, QKV, AG, PR, IV, AT, FA, ST, SS, RD, NG,
    LN, LA, SN, SA, RP, RO, G, r1, r2, r3,
    wsem, osem, s_sp, r_sp, s_h, r_h, s_q, r_q, s_a, r_a, s_st, r_st, s_rd, r_rd,
    s_l, r_l, s_o, r_o, s_pj, r_pj, ss, rs, s_far, r_far,
):
    sec = lax.axis_index("section")
    view = lax.axis_index("view")
    zi = lax.axis_index("dp")
    core = lax.rem(view, 2)
    yi = lax.rem(view // 2, 4)
    xi = view // 8
    micros, toks, width = x_hbm.shape
    heads = width // HEAD_DIM
    relay = 3 - core
    scale_log2 = scale * math.log2(math.e)
    f32, bf = jnp.float32, jnp.bfloat16

    peer = {"view": view + 1 - 2 * core}
    ahead = {"view": lax.rem(view + 2, 16)}
    behind = {"view": lax.rem(view + 14, 16)}
    diag = {"view": lax.rem(view + 15 + 2 * core, 16)}
    other = {"section": 1 - sec}
    across = {"view": lax.rem(view + 8, 16)}

    def y_dev(step):
        return {"view": xi * 8 + lax.rem(yi + step + 4, 4) * 2 + core}

    def z_dev(step):
        return {"dp": lax.rem(zi + step + 4, 4)}

    loads = [
        pltpu.make_async_copy(win_hbm, win, wsem.at[0]),
        pltpu.make_async_copy(wout_hbm, wout, wsem.at[1]),
    ]
    own_in = [
        [pltpu.make_async_copy(x_hbm.at[m], X.at[m, 0], wsem.at[2 + m]) for m in range(micros)],
        [pltpu.make_async_copy(cot_hbm.at[m], OG.at[m, 0], wsem.at[2 + m]) for m in range(micros)],
    ]
    for s in range(2):
        @pl.when(sec == s)
        def _():
            for copy in own_in[s]:
                copy.start()

    for load in loads:
        load.start()

    partners = (
        peer, ahead, behind, diag, other, across, y_dev(1), y_dev(2), y_dev(3), z_dev(1),
        z_dev(2), z_dev(3),
    ) + tuple(
        dict(across, dp=lax.rem(zi + step, 4)) for step in range(1, 4)
    ) + tuple(
        {"view": (1 - xi) * 8 + lax.rem(yi + step, 4) * 2 + core} for step in range(1, 4)
    )
    barrier = pltpu.get_barrier_semaphore()
    for dev in partners:
        pl.semaphore_signal(barrier, inc=1, device_id=dev, device_id_type=MESH)
    pl.semaphore_wait(barrier, len(partners))

    def remote(src, dst, s, r, dev):
        return pltpu.make_async_remote_copy(
            src_ref=src, dst_ref=dst, send_sem=s, recv_sem=r, device_id=dev, device_id_type=MESH
        )

    def when_section(s):
        return pl.when(sec == s)

    step = toks // PIECES

    def spread(t, m, way, i):
        buf = (X, OG)[t]
        rows = pl.ds(i * step, step)
        return remote(
            buf.at[m, 0, rows], buf.at[m, 1 + way, rows],
            s_sp.at[t, m, way, i], r_sp.at[t, m, way, i], (ahead, behind)[way],
        )

    def hop(t, m, i):
        src, dst = ((out_ref, X), (grad_ref, OG))[t]
        rows = pl.ds(i * step, step)
        return remote(
            src.at[m, rows], dst.at[m, 0, rows], s_h.at[m, i], r_h.at[m, i], other
        )

    def share_qkv(m, which, j):
        src, dst = ((0, 1), (relay, 4))[which]
        cols = pl.ds(j * width, width)
        return remote(
            QKV.at[m, src, :, cols], QKV.at[m, dst, :, cols],
            s_q.at[m, which, j], r_q.at[m, which, j], peer,
        )

    def share_ag(m, which):
        src, dst = ((0, 1), (relay, 4))[which]
        return remote(AG.at[m, src], AG.at[m, dst], s_a.at[m, which], r_a.at[m, which], peer)

    ROUTES = {1: (1, peer), 3: (2, behind), 2: (3, ahead), 4: (4, diag)}

    def stats_to(m, block):
        target, dev = ROUTES[block]
        return remote(
            SS.at[m, target - 1], ST.at[m, block],
            s_st.at[m, block - 1], r_st.at[m, block - 1], dev,
        )

    def dots_to(m, block):
        return remote(
            RD.at[m, 0], RD.at[m, block],
            s_rd.at[m, block - 1], r_rd.at[m, block - 1], ROUTES[block][1],
        )

    own_toks = micros * toks

    def share_left(which):
        src, dst = ((SN, LN), (SA, LA))[which]
        return remote(
            src, dst.at[:, :, pl.ds(own_toks, own_toks)], s_l.at[which], r_l.at[which], peer
        )

    def share_og(m):
        return remote(RO.at[m], RO.at[micros + m], s_o.at[m], r_o.at[m], peer)

    def share_proj(m, which):
        half = width // 2
        cols = (
            pl.ds(0, width), pl.ds(width, half), pl.ds(2 * width, half),
            pl.ds(width + half, half), pl.ds(2 * width + half, half),
        )[which]
        return remote(
            RP.at[m, :, cols], RP.at[micros + m, :, cols],
            s_pj.at[m, which], r_pj.at[m, which], peer,
        )

    def start_spread(t, m):
        for i in range(PIECES):
            spread(t, m, 0, i).start()
            spread(t, m, 1, i).start()

    def wait_spread(t, m):
        for i in range(PIECES):
            spread(t, m, 0, i).wait_recv()
            spread(t, m, 1, i).wait_recv()

    def pass_piece(t, m, i):
        hop(t, m, i).wait_recv()
        spread(t, m, 0, i).start()
        spread(t, m, 1, i).start()

    def receive_hop(t, m):
        for i in range(PIECES):
            pass_piece(t, m, i)

    def store(which, m):
        src, dst = ((out_ref, out_hbm), (grad_ref, grad_hbm))[which]
        return pltpu.make_async_copy(src.at[m], dst.at[m], osem.at[which, m])

    def store_grads(which):
        src, dst = ((gin, gin_hbm), (gout, gout_hbm))[which]
        return pltpu.make_async_copy(src, dst, osem.at[2, which])

    side = 1 - 2 * core
    offsets = (0, side, -2, 2, -side)

    def live_block(m, k):
        if k == 0:
            return jnp.ones((1, toks), f32)
        live = jnp.float32(0.0)
        for j in range(nbr_ref.shape[1]):
            rel = lax.rem(nbr_ref[m, j] - view - offsets[k] + 32, 16)
            hit = jnp.logical_and(rel == 0, j < cnt_ref[m])
            live = jnp.where(hit, jnp.float32(1.0), live)
        return jnp.full((1, toks), live, f32)

    def norm_block(m, at):
        rows = X[m, at].astype(f32)
        factor = lax.rsqrt(jnp.mean(rows * rows, -1, keepdims=True) + EPSILON)
        normed = (rows * factor).astype(bf)
        N[at] = normed
        return factor, normed

    def keep_left(value, mine, theirs, m):
        parts = value.T.reshape(8, 2, width // 16, toks)
        cols = slice(m * toks, (m + 1) * toks)
        first, second = parts[:, 0], parts[:, 1]
        mine[:, :, cols] = jnp.where(core == 0, first, second)
        theirs[:, :, cols] = jnp.where(core == 0, second, first)

    def lanes():
        return lax.broadcasted_iota(jnp.int32, (toks, HEAD_DIM), 1)

    def project_own(m):
        factor, normed = norm_block(m, 0)
        FA[m] = factor
        for j in (1, 2, 0):
            cols = slice(j * width, (j + 1) * width)
            QKV[m, 0, :, cols] = jnp.dot(
                N[0], win[:, cols], preferred_element_type=f32
            ).astype(bf)
            share_qkv(m, 0, j).start()
        keep_left(normed, LN, SN, m)

    def forward(m):
        wait_spread(0, m)
        if m == 0:
            @when_section(0)
            def _():
                start_spread(0, 1)

        norm_block(m, 1)
        norm_block(m, 2)
        for block, shared in ((relay, True), (5 - relay, False)):
            for j in (1, 2):
                cols = slice(j * width, (j + 1) * width)
                QKV[m, block, :, cols] = jnp.dot(
                    N[block - 1], win[:, cols], preferred_element_type=f32
                ).astype(bf)
                if shared:
                    share_qkv(m, 1, j).start()
        near = jnp.dot(
            N[1:3].reshape(2 * toks, width), win[:, :width], preferred_element_type=f32
        ).astype(bf)
        QKV[m, 2:4, :, :width] = near.reshape(2, toks, width)
        share_qkv(m, 1, 0).start()
        for j in (1, 2):
            share_qkv(m, 0, j).wait_recv()
            share_qkv(m, 1, j).wait_recv()
        lives = [live_block(m, k) for k in range(BLOCKS)]
        live = jnp.concatenate(lives, 1) > 0.0
        stats = jnp.zeros((toks, HEAD_DIM), f32)
        for h in range(heads):
            cols = slice(h * HEAD_DIM, (h + 1) * HEAD_DIM)
            kcols = slice(width + h * HEAD_DIM, width + (h + 1) * HEAD_DIM)
            vcols = slice(2 * width + h * HEAD_DIM, 2 * width + (h + 1) * HEAD_DIM)
            scores = lax.dot_general(
                QKV[m, 0, :, cols], QKV[m, :, :, kcols].reshape(BLOCKS * toks, HEAD_DIM), LAST,
                preferred_element_type=f32,
            )
            masked = jnp.where(live, scores, NEGATIVE)
            top = jnp.max(masked, -1, keepdims=True)
            terms = jnp.exp2((masked - top) * scale_log2)
            inverse = 1.0 / jnp.sum(terms, -1, keepdims=True)
            low = terms.astype(bf)
            PR[m, h] = low
            IV[m, h] = inverse
            AT[m, :, cols] = (
                jnp.dot(
                    low, QKV[m, :, :, vcols].reshape(BLOCKS * toks, HEAD_DIM),
                    preferred_element_type=f32,
                ) * inverse
            ).astype(bf)
            stats = jnp.where(lanes() == h, top, stats)
            stats = jnp.where(lanes() == heads + h, inverse, stats)
            if m == 0 and h % 2 == 1:
                @when_section(1)
                def _():
                    pass_piece(0, 1, h // 2)
        if m == 0:
            @when_section(0)
            def _():
                loads[1].wait()

        branch = jnp.dot(AT[m], wout[...], preferred_element_type=f32)
        out_ref[m] = (X[m, 0].astype(f32) + branch).astype(bf)
        store(0, m).start()

        @when_section(0)
        def _():
            for i in range(PIECES):
                hop(0, m, i).start()

        turned = stats.T
        ST[m, 0] = turned[: 2 * heads]
        for k in range(1, BLOCKS):
            SS[m, k - 1, :heads] = jnp.where(lives[k] > 0.0, turned[:heads], -NEGATIVE)
            SS[m, k - 1, heads:] = turned[heads : 2 * heads]
        for block in ROUTES:
            stats_to(m, block).start()
        keep_left(AT[m], LA, SA, m)

    def own_ag(m):
        AG[m, 0] = lax.dot_general(
            OG[m, 0], wout[...], LAST, preferred_element_type=f32
        ).astype(bf)
        share_ag(m, 0).start()

    def near_ag(m):
        wait_spread(1, m)
        near = lax.dot_general(
            OG[m, 1:3].reshape(2 * toks, width), wout[...], LAST, preferred_element_type=f32
        ).astype(bf)
        AG[m, 2:4] = near.reshape(2, toks, width)
        share_ag(m, 1).start()

    def query_side(m):
        dots = jnp.zeros((toks, HEAD_DIM), f32)
        row_dots = []
        for h in range(heads):
            cols = slice(h * HEAD_DIM, (h + 1) * HEAD_DIM)
            row_dots.append(
                jnp.sum(
                    AG[m, 0, :, cols].astype(f32) * AT[m, :, cols].astype(f32), -1, keepdims=True
                )
            )
            dots = jnp.where(lanes() == h, row_dots[h], dots)
        RD[m, 0] = dots.T[:heads]
        for block in ROUTES:
            dots_to(m, block).start()
        RO[m] = OG[m, 0]
        share_og(m).start()
        for h in range(heads):
            cols = slice(h * HEAD_DIM, (h + 1) * HEAD_DIM)
            kcols = slice(width + h * HEAD_DIM, width + (h + 1) * HEAD_DIM)
            vcols = slice(2 * width + h * HEAD_DIM, 2 * width + (h + 1) * HEAD_DIM)
            terms = PR[m, h].astype(f32)
            prob_grad = lax.dot_general(
                AG[m, 0, :, cols], QKV[m, :, :, vcols].reshape(BLOCKS * toks, HEAD_DIM), LAST,
                preferred_element_type=f32,
            )
            score_grad = (terms * (prob_grad - row_dots[h])).astype(bf)
            RP[m, :, cols] = (
                jnp.dot(
                    score_grad, QKV[m, :, :, kcols].reshape(BLOCKS * toks, HEAD_DIM),
                    preferred_element_type=f32,
                ) * (IV[m, h] * scale)
            ).astype(bf)
        share_proj(m, 0).start()

    def backward(m):
        last = m == micros - 1

        @when_section(0)
        def _():
            receive_hop(1, m)
            own_ag(m)
            if m == 0:
                query_side(m)

        if m > 0:
            query_side(m)

        @when_section(0)
        def _():
            if last:
                open_pair(0)
            near_ag(m)
            if last:
                open_pair(1)
                stage(0, 1)

        for which in range(2):
            share_qkv(m, which, 0).wait_recv()
            share_ag(m, which).wait_recv()
        for block in ROUTES:
            stats_to(m, block).wait_recv()
            dots_to(m, block).wait_recv()

        def row(ref, h):
            return jnp.concatenate([ref[m, k, h : h + 1, :] for k in range(BLOCKS)], 1)

        for h in range(heads):
            cols = slice(h * HEAD_DIM, (h + 1) * HEAD_DIM)
            kcols = slice(width + h * HEAD_DIM, width + (h + 1) * HEAD_DIM)
            vcols = slice(2 * width + h * HEAD_DIM, 2 * width + (h + 1) * HEAD_DIM)
            queries = QKV[m, :, :, cols].reshape(BLOCKS * toks, HEAD_DIM)
            out_grads = AG[m, :, :, cols].reshape(BLOCKS * toks, HEAD_DIM)
            scores = lax.dot_general(
                QKV[m, 0, :, kcols], queries, LAST, preferred_element_type=f32
            )
            prob = jnp.exp2((scores - row(ST, h)) * scale_log2) * row(ST, heads + h)
            prob_grad = lax.dot_general(
                QKV[m, 0, :, vcols], out_grads, LAST, preferred_element_type=f32
            )
            score_grad = (prob * (prob_grad - row(RD, h))).astype(bf)
            RP[m, :, kcols] = (
                jnp.dot(score_grad, queries, preferred_element_type=f32) * scale
            ).astype(bf)
            RP[m, :, vcols] = jnp.dot(
                prob.astype(bf), out_grads, preferred_element_type=f32
            ).astype(bf)
            if h == heads // 2 - 1 or h == heads - 1:
                piece = 1 + 2 * (h // (heads // 2))
                share_proj(m, piece).start()
                share_proj(m, piece + 1).start()
            if last and h == heads // 2 - 1:
                @when_section(0)
                def _():
                    stage(1, 1)

    def finish(m):
        NG[...] = jnp.dot(RP[m], winT[...], preferred_element_type=f32)
        normed_grad = NG[...]
        factor = FA[m]
        unit = X[m, 0].astype(f32) * factor
        inner = jnp.mean(normed_grad * unit, -1, keepdims=True)
        grad_ref[m] = (
            OG[m, 0].astype(f32) + factor * (normed_grad - unit * inner)
        ).astype(bf)
        store(1, m).start()

    whole = slice(None)
    ring_at = (yi, zi)
    far_at = (zi, yi)

    def turn(value, by):
        return lax.rem(value + by, 4)

    def first(t, p, x_at, a):
        return G.at[t, p, x_at, a] if t == 0 else G.at[t, p, x_at, :, a]

    def second(t, p, x_at, b):
        a = ring_at[t]
        return G.at[t, p, x_at, a, b] if t == 0 else G.at[t, p, x_at, b, a]

    def far_dev(t, dx, db):
        x_to = xi if dx == 0 else 1 - xi
        if t == 0:
            return {"view": x_to * 8 + yi * 2 + core, "dp": turn(zi, db)}
        return {"view": x_to * 8 + turn(yi, db) * 2 + core}

    def ring(t, p, s):
        a = ring_at[t]
        dev = (y_dev, z_dev)[t]

        def make(k, src, dst, to):
            return remote(src, dst, ss.at[t, p, k], rs.at[t, p, k], to)

        if s == 0:
            return (
                make(0, first(t, p, 0, turn(a, 2)), r1.at[t, p, 0], dev(1)),
                make(1, first(t, p, 1, turn(a, 2)), r1.at[t, p, 1], dev(-1)),
            )
        return (
            make(2, first(t, p, whole, turn(a, 1)), r2.at[t, p, 0], dev(1)),
            make(3, first(t, p, whole, turn(a, 3)), r2.at[t, p, 1], dev(-1)),
        )

    def far(t, batch, k):
        dx, db = FAR[k]
        x_to = xi if dx == 0 else 1 - xi
        both = pl.ds(2 * batch, 2)
        return remote(
            second(t, both, x_to, turn(far_at[t], db)), r3.at[t, k, both],
            s_far.at[t, batch, k], r_far.at[t, batch, k], far_dev(t, dx, db),
        )

    def add_into(ref, *others):
        total = ref[...].astype(f32)
        for item in others:
            total = total + item[...].astype(f32)
        ref[...] = total.astype(bf)

    def stage(p, s):
        for t in range(2):
            n = PAIRS[p][t]
            a = ring_at[t]
            if s > 0:
                for copy in ring(t, p, s - 1):
                    copy.wait_recv()
            if s == 0:
                left = LA if n >= 6 else LN
                right, k = (RO, n - 6) if n >= 6 else (RP, n)
                part = jnp.dot(
                    left[...].reshape(left.shape[0] * left.shape[1], 2 * own_toks),
                    right[:, :, k * CHUNK : (k + 1) * CHUNK].reshape(2 * own_toks, CHUNK),
                    preferred_element_type=f32,
                )
                G[t, p] = part.astype(bf).reshape(G.shape[2:])
            elif s == 1:
                add_into(first(t, p, 0, turn(a, 1)), r1.at[t, p, 0])
                add_into(first(t, p, 1, turn(a, 3)), r1.at[t, p, 1])
            else:
                add_into(first(t, p, whole, a), r2.at[t, p, 0], r2.at[t, p, 1])
            if s < 2:
                for copy in ring(t, p, s):
                    copy.start()

    def send_far(batch):
        for t in range(2):
            for k in range(len(FAR)):
                far(t, batch, k).start()

    def take_far(batch):
        for t in range(2):
            for k in range(len(FAR)):
                far(t, batch, k).wait_recv()
            for p in (2 * batch, 2 * batch + 1):
                total = second(t, p, xi, far_at[t])[...].astype(f32)
                for k in range(len(FAR)):
                    total = total + r3[t, k, p].astype(f32)
                n = PAIRS[p][t]
                out, c = (gin, n) if n < 6 else (gout, n - 6)
                out[:, c * CHUNK : (c + 1) * CHUNK] = total * share

    def open_pair(p):
        if p == 0:
            for m in range(micros):
                share_og(m).wait_recv()
            share_left(1).wait_recv()
        elif p == 1:
            share_left(0).wait_recv()
            for m in range(micros):
                share_proj(m, 0).wait_recv()
        else:
            for m in range(micros):
                share_proj(m, 2 * p - 3).wait_recv()
                share_proj(m, 2 * p - 2).wait_recv()
        stage(p, 0)

    def turn_weights():
        @pl.loop(0, 3 * width // HEAD_DIM)
        def _(j):
            at = pl.ds(pl.multiple_of(j * HEAD_DIM, HEAD_DIM), HEAD_DIM)
            winT[at, :] = win[:, at].T

    @when_section(0)
    def _():
        for copy in own_in[0]:
            copy.wait()
        start_spread(0, 0)

    @when_section(1)
    def _():
        for m in range(micros):
            own_in[1][m].wait()
            start_spread(1, m)

    loads[0].wait()

    @when_section(1)
    def _():
        loads[1].wait()
        for m in range(micros):
            own_ag(m)
            near_ag(m)
        turn_weights()

    @when_section(1)
    def _():
        receive_hop(0, 0)

    project_own(0)

    @when_section(0)
    def _():
        project_own(1)

    forward(0)

    @when_section(1)
    def _():
        project_own(1)
        query_side(0)

    forward(1)

    @when_section(0)
    def _():
        turn_weights()

    for which in range(2):
        share_left(which).start()
    for m in range(micros):
        backward(m)
        if m < micros - 1:
            finish(m)

            @when_section(1)
            def _():
                for i in range(PIECES):
                    hop(1, m, i).start()

    @when_section(1)
    def _():
        finish(micros - 1)
        for i in range(PIECES):
            hop(1, micros - 1, i).start()
        open_pair(0)
        open_pair(1)
        stage(0, 1)
        stage(1, 1)

    open_pair(2)
    open_pair(3)

    @when_section(0)
    def _():
        finish(micros - 1)

    stage(2, 1)
    stage(3, 1)
    stage(0, 2)
    stage(1, 2)
    send_far(0)
    stage(2, 2)
    stage(3, 2)
    send_far(1)
    take_far(0)
    take_far(1)
    for which in range(2):
        store_grads(which).start()

    for which in range(2):
        for m in range(micros):
            store(which, m).wait()
        store_grads(which).wait()
    for m in range(micros):
        for t in range(2):
            for i in range(PIECES):
                spread(t, m, 0, i).wait_send()
                spread(t, m, 1, i).wait_send()
        for i in range(PIECES):
            @when_section(0)
            def _():
                hop(0, m, i).wait_send()

            @when_section(1)
            def _():
                hop(1, m, i).wait_send()
        for which in range(2):
            for j in range(3):
                share_qkv(m, which, j).wait_send()
            share_ag(m, which).wait_send()
        for which in range(5):
            share_proj(m, which).wait_send()
        for block in ROUTES:
            stats_to(m, block).wait_send()
            dots_to(m, block).wait_send()
        share_og(m).wait_send()
    for which in range(2):
        share_left(which).wait_send()
    for t in range(2):
        for p in range(len(PAIRS)):
            for s in range(2):
                for copy in ring(t, p, s):
                    copy.wait_send()
        for batch in range(2):
            for k in range(len(FAR)):
                far(t, batch, k).wait_send()


def hand_over_kernel(*refs):
    count = len(refs) // 2
    for i in range(count):
        refs[count + i][...] = refs[i][...]


def hand_over(*arrays):
    vm = pl.BlockSpec(memory_space=pltpu.VMEM)
    return pl.pallas_call(
        hand_over_kernel,
        out_shape=tuple(jax.ShapeDtypeStruct(a.shape, a.dtype) for a in arrays),
        in_specs=[vm] * len(arrays),
        out_specs=(vm,) * len(arrays),
    )(*arrays)


def on_device(scenes, neighbours, counts, w_in, w_out, cotangent):
    micros, _, toks, width = scenes.shape
    heads = width // HEAD_DIM
    share = 1.0 / (micros * lax.axis_size("dp"))
    pairs = len(PAIRS)
    rows = width // 64
    group = width // 16
    vm = pl.BlockSpec(memory_space=pltpu.VMEM)
    sm = pl.BlockSpec(memory_space=pltpu.SMEM)
    hbm = pl.BlockSpec(memory_space=pl.ANY)
    bf, f32 = jnp.bfloat16, jnp.float32
    sds = jax.ShapeDtypeStruct
    dma = pltpu.SemaphoreType.DMA
    outputs, grads, grad_in, grad_out = pl.pallas_call(
        functools.partial(scene_kernel, 1.0 / math.sqrt(HEAD_DIM), share),
        out_shape=(
            sds((micros, toks, width), bf),
            sds((micros, toks, width), bf),
            sds((rows, 3 * width), f32),
            sds((rows, width), f32),
        ),
        in_specs=[hbm, hbm, sm, sm, hbm, hbm],
        out_specs=(hbm,) * 4,
        scratch_shapes=[
            pltpu.VMEM((micros, toks, width), bf),
            pltpu.VMEM((micros, toks, width), bf),
            pltpu.VMEM((rows, 3 * width), f32),
            pltpu.VMEM((rows, width), f32),
            pltpu.VMEM((width, 3 * width), bf),
            pltpu.VMEM((3 * width, width), bf),
            pltpu.VMEM((width, width), bf),
            pltpu.VMEM((micros, 3, toks, width), bf),
            pltpu.VMEM((micros, 3, toks, width), bf),
            pltpu.VMEM((3, toks, width), bf),
            pltpu.VMEM((micros, BLOCKS, toks, 3 * width), bf),
            pltpu.VMEM((micros, BLOCKS, toks, width), bf),
            pltpu.VMEM((micros, heads, toks, BLOCKS * toks), bf),
            pltpu.VMEM((micros, heads, toks, 1), f32),
            pltpu.VMEM((micros, toks, width), bf),
            pltpu.VMEM((micros, toks, 1), f32),
            pltpu.VMEM((micros, BLOCKS, 2 * heads, toks), f32),
            pltpu.VMEM((micros, BLOCKS - 1, 2 * heads, toks), f32),
            pltpu.VMEM((micros, BLOCKS, heads, toks), f32),
            pltpu.VMEM((toks, width), f32),
            pltpu.VMEM((8, group, 2 * micros * toks), bf),
            pltpu.VMEM((8, group, 2 * micros * toks), bf),
            pltpu.VMEM((8, group, micros * toks), bf),
            pltpu.VMEM((8, group, micros * toks), bf),
            pltpu.VMEM((2 * micros, toks, 3 * width), bf),
            pltpu.VMEM((2 * micros, toks, width), bf),
            pltpu.VMEM((2, pairs, 2, 4, 4, rows, CHUNK), bf),
            pltpu.VMEM((2, pairs, 2, 4, rows, CHUNK), bf),
            pltpu.VMEM((2, pairs, 2, 2, 4, rows, CHUNK), bf),
            pltpu.VMEM((2, len(FAR), pairs, rows, CHUNK), bf),
            dma((2 + micros,)),
            dma((3, 2)),
            dma((2, micros, 2, PIECES)), dma((2, micros, 2, PIECES)),
            dma((micros, PIECES)), dma((micros, PIECES)),
            dma((micros, 2, 3)), dma((micros, 2, 3)),
            dma((micros, 2)), dma((micros, 2)),
            dma((micros, 4)), dma((micros, 4)),
            dma((micros, 4)), dma((micros, 4)),
            dma((2,)), dma((2,)),
            dma((micros,)), dma((micros,)),
            dma((micros, 5)), dma((micros, 5)),
            dma((2, pairs, 4)), dma((2, pairs, 4)),
            dma((2, 2, len(FAR))), dma((2, 2, len(FAR))),
        ],
        compiler_params=pltpu.CompilerParams(
            collective_id=1, has_side_effects=True, vmem_limit_bytes=62 * 1024 * 1024
        ),
        cost_estimate=pl.CostEstimate(
            flops=20 * 10**9, bytes_accessed=12 << 20, transcendentals=2 * 10**6
        ),
    )(scenes[:, 0], cotangent[:, 0], neighbours[:, 0], counts[:, 0], w_in[0], w_out[0])
    outputs, grads, grad_in, grad_out = hand_over(outputs, grads, grad_in, grad_out)
    return (outputs[None, :, None], grads[None, :, None], grad_in[None], grad_out[None])


def solution(mesh):
    in_specs = (
        P("dp", "view", None, None),
        P("dp", "view", None),
        P("dp", "view"),
        P("section", None, None),
        P("section", None, None),
        P("dp", "view", None, None),
    )
    out_specs = (
        P("section", "dp", "view", None, None),
        P("section", "dp", "view", None, None),
        P("section", ("view", "dp"), None),
        P("section", ("view", "dp"), None),
    )
    return jax.shard_map(
        on_device, mesh=mesh, in_specs=in_specs, out_specs=out_specs, check_vma=False
    )
```

time: 152 us -> 119 us (0.78)
  Pallas kernels: 143 us -> 118 us
  local copies, waits for them, and re-layouts: 8.12 us -> 0 us
    pallas_call x1, Pallas kernels: 143 us -> 116 us  [on_device(): pl.pallas_call(functools.partial(scene_kernel, 1.0 / math.sqrt(HEAD_DIM),...]
    unnamed x5 -> x0, local copies, waits for them, and re-layouts: 8.12 us -> none
    pallas_call x0 -> x1, Pallas kernels: none -> 2.32 us  [hand_over(): pl.pallas_call(hand_over_kernel, out_shape=tuple((jax.ShapeDtypeStruct(a....]
where the time goes in v4:
time: 119 us
  Pallas kernels  118 us (99%)
    pallas_call x1, Pallas kernels, on_device(): pl.pallas_call(functools.partial(scene_kernel, 1.0 / math.sqrt(HEAD_DIM),...  116 us

profile of v4, /device:TPU:0, one launch (start us, length us, event | category | flops | bytes accessed | tf_op | source)
XLA Modules:
  0.0 118.8 jit_solution(896105770133317118)
XLA Ops:
  0.6 115.8 %shard_map.93 = (bf16[2,128,1024]{2,1,0:T(8,128)(2,1)}, bf16[2,128,1024]{2,1,0:T(8,128)(2,1)}, f32[16,3072]{1,0:T(8,128)}, f32[16,1024]{1,0:T(8,128)}) custom-call(bf16[2,128,1024]{2,1,0:T(8,128)(2,1)} %bitcast.16, bf16[2,128,1024]{2,1,0:T(8,128)(2,1)} %bitcast.17, s32[2,3]{1,0:T(2,128)} %bitcast.22, s32[2]{0:T(128)} %bitcast.23, ...), custom_call_target="tpu_custom_call" | custom-call | flops 20000000000 | bytes 12582912 | tf_op jit(solution)/shard_map/pallas_call | solution.py:697
  116.5 2.3 %shard_map.94 = (bf16[2,128,1024]{2,1,0:T(8,128)(2,1)}, bf16[2,128,1024]{2,1,0:T(8,128)(2,1)}, f32[16,3072]{1,0:T(8,128)}, f32[16,1024]{1,0:T(8,128)}) custom-call(bf16[2,128,1024]{2,1,0:T(8,128)(2,1)} %get-tuple-element.12.refs_0_, bf16[2,128,1024]{2,1,0:T(8,128)(2,1)} %get-tuple-element.13.refs_1_, f32[16,3072]{1,0:T(8,128)} %get-tuple-element.14.refs_2_, ...), custom_call_target="tpu_custom_call" | custom-call | tf_op jit(solution)/shard_map/pallas_call | solution.py:676
